TPU v7x, 512 devices: a whole 4x8x8 slice. The times are simulated.
512 devices in a mesh: outer: 16 (over z, core), inner: 32 (over x, y).
Axes of the slice: x: 4, y: 8, z: 8, core: 2. Of those that a mesh axis runs over, the one named last changes fastest.
Arguments:
- queries: bfloat16 [65536, 1024], P(('outer', 'inner')), may hold values from -16 to 16
- keys: bfloat16 [65536, 128], P(('outer', 'inner')), may hold values from -8 to 8
- values: bfloat16 [65536, 128], P(('outer', 'inner')), may hold values from -6 to 6
- d_out: bfloat16 [65536, 1024], P(('outer', 'inner')), may hold values from -6 to 6
- doc_ids: int32 [65536], replicated, may hold values from 0 to 63, never falling along the last dimension, each value on 1 to 2048 neighbouring positions
Outputs:
- attended: bfloat16 [65536, 1024], P(('outer', 'inner'))
- grad_queries: bfloat16 [65536, 1024], P(('outer', 'inner'))
- grad_keys: bfloat16 [65536, 128], P(('outer', 'inner'))
- grad_values: bfloat16 [65536, 128], P(('outer', 'inner'))
Inputs may be any that keep to these rules, and one draw needn't show every extreme that they name: `doc_ids`: never falls along the sequence; each document holds 1 to 2048 tokens, one exactly 2048.
All inputs are finite; a program needn't handle non-finite values.
Results may differ from a plain program's by a relative error of at most 0.012.
The roundings to bfloat16 on the way count: a program that leaves them out, or rounds other values in their place, can miss the bound.
Values may be sent and summed in bfloat16 or wider, within the bound.
No kernel may reach another device: no remote copies, remote signals or barrier semaphores. Data moves between devices by JAX's collectives and lax.ppermute only.
A program may use at most 64 MiB of HBM per device.

v0:
```python
import math

import jax
import jax.numpy as jnp
from jax import lax
from jax.sharding import PartitionSpec as P

WINDOW = 1024


LOW_START = -1e30


def from_behind(block, axis, distance):
    devices = range(lax.axis_size(axis))
    route = [(i - distance, i) for i in devices if i - distance in devices]
    return lax.ppermute(block, axis, route)


def contract_last(left_op, right_op):
    return lax.dot_general(
        left_op, right_op, (((1,), (1,)), ((), ())), preferred_element_type=jnp.float32
    )


def contract_first(left_op, right_op):
    return lax.dot_general(
        left_op, right_op, (((0,), (0,)), ((), ())), preferred_element_type=jnp.float32
    )


def body(queries, keys, values, d_out, doc_ids):
    n_inner = lax.axis_size("inner")
    me_inner = lax.axis_index("inner")
    me_flat = lax.axis_index("outer") * n_inner + me_inner
    tokens = keys.shape[0]
    head_width = keys.shape[1]
    head_count = queries.shape[1] // head_width
    score_scale = 1.0 / math.sqrt(head_width)
    reach = WINDOW // tokens
    span = reach * tokens
    levels = reach.bit_length() - 1
    packed = jnp.concatenate([keys, values], axis=1)
    pieces = [packed]
    for distance in range(1, reach):
        pieces = [from_behind(packed, ("outer", "inner"), distance)] + pieces
    window_kv = jnp.concatenate(pieces, axis=0)
    first_pos = (me_flat - reach + 1) * tokens
    key_pos = first_pos + jnp.arange(span, dtype=jnp.int32)
    key_doc = jnp.take(doc_ids, jnp.clip(key_pos, 0, doc_ids.shape[0] - 1))
    query_doc = lax.dynamic_slice_in_dim(doc_ids, me_flat * tokens, tokens)
    row_pos = jnp.repeat(me_flat * tokens + jnp.arange(tokens, dtype=jnp.int32), head_count)
    row_doc = jnp.repeat(query_doc, head_count)
    n_rows = tokens * head_count
    query_rows = queries.reshape(n_rows, head_width)
    grad_rows = d_out.reshape(n_rows, head_width)
    tile = min(span, 512)
    n_tiles = span // tile
    kv_tiles = window_kv.reshape(n_tiles, tile, 2 * head_width)
    pos_tiles = key_pos.reshape(n_tiles, tile)
    doc_tiles = key_doc.reshape(n_tiles, tile)

    def tile_scores(kv_blk, pos_blk, doc_blk):
        raw_scores = contract_last(query_rows, kv_blk[:, :head_width]) * score_scale
        visible = (
            (pos_blk[None, :] <= row_pos[:, None])
            & (pos_blk[None, :] >= 0)
            & (doc_blk[None, :] == row_doc[:, None])
        )
        return jnp.where(visible, raw_scores, -jnp.inf)

    def forward_tile(state_now, slab):
        kv_blk, pos_blk, doc_blk = slab
        row_top, row_total, row_accum = state_now
        masked = tile_scores(kv_blk, pos_blk, doc_blk)
        new_top = jnp.maximum(row_top, jnp.max(masked, axis=1))
        weights = jnp.exp(masked - new_top[:, None])
        rescale = jnp.exp(row_top - new_top)
        row_total = row_total * rescale + jnp.sum(weights, axis=1)
        row_accum = row_accum * rescale[:, None] + jnp.dot(
            weights, kv_blk[:, head_width:].astype(jnp.float32), precision=lax.Precision.HIGHEST
        )
        return ((new_top, row_total, row_accum), None)

    start_state = (
        jnp.full((n_rows,), LOW_START, jnp.float32),
        jnp.zeros((n_rows,), jnp.float32),
        jnp.zeros((n_rows, head_width), jnp.float32),
    )
    (row_top, row_total, row_accum), _ = lax.scan(
        forward_tile, start_state, (kv_tiles, pos_tiles, doc_tiles)
    )
    output_full = row_accum / row_total[:, None]
    attended = output_full.reshape(tokens, head_count * head_width).astype(jnp.bfloat16)
    deltas = jnp.sum(grad_rows.astype(jnp.float32) * output_full, axis=1)

    def backward_tile(query_grad, slab):
        kv_blk, pos_blk, doc_blk = slab
        key_blk = kv_blk[:, :head_width]
        value_blk = kv_blk[:, head_width:]
        probs = (
            jnp.exp(tile_scores(kv_blk, pos_blk, doc_blk) - row_top[:, None]) / row_total[:, None]
        )
        probs_low = probs.astype(jnp.bfloat16)
        value_grad = contract_first(probs_low, grad_rows)
        prob_grad = contract_last(grad_rows, value_blk)
        score_grad = (probs * (prob_grad - deltas[:, None]) * score_scale).astype(jnp.bfloat16)
        query_grad = query_grad + jnp.dot(score_grad, key_blk, preferred_element_type=jnp.float32)
        key_grad = contract_first(score_grad, query_rows)
        return (query_grad, jnp.concatenate([key_grad, value_grad], axis=1))

    start_grad = jnp.zeros((n_rows, head_width), jnp.float32)
    query_grad, kv_terms = lax.scan(backward_tile, start_grad, (kv_tiles, pos_tiles, doc_tiles))
    grad_queries = query_grad.reshape(tokens, head_count * head_width).astype(jnp.bfloat16)
    gathered = kv_terms.reshape(span, 2 * head_width)
    for level in reversed(range(levels)):
        step_rows = (1 << level) * tokens
        lower = gathered[:step_rows]
        upper = gathered[step_rows:]
        gathered = upper + from_behind(lower, ("outer", "inner"), -(1 << level))
    grad_keys = gathered[:, :head_width].astype(jnp.bfloat16)
    grad_values = gathered[:, head_width:].astype(jnp.bfloat16)
    return (attended, grad_queries, grad_keys, grad_values)


def solution(mesh):
    return jax.shard_map(
        body,
        mesh=mesh,
        in_specs=(
            P(("outer", "inner"), None),
            P(("outer", "inner"), None),
            P(("outer", "inner"), None),
            P(("outer", "inner"), None),
            P(),
        ),
        out_specs=(
            P(("outer", "inner"), None),
            P(("outer", "inner"), None),
            P(("outer", "inner"), None),
            P(("outer", "inner"), None),
        ),
        check_vma=False,
    )
```

profile of v0, /device:TPU:255, one launch (start us, length us, event | category | flops | bytes accessed | tf_op | source)
XLA Modules:
  0.0 129.8 jit_solution(17732360305157059363)
XLA Ops:
  0.6 0.8 constant_dynamic-update-slice_fusion.2
  1.4 0.8 constant_dynamic-update-slice_fusion.1
  2.2 4.9 %collective-permute-start.6 = (bf16[128,256]{1,0:T(8,128)(2,1)S(1)}, bf16[128,256]{1,0:T(8,128)(2,1)S(1)}, u32[]{:S(2)}, u32[]{:S(2)}) collective-permute-start(bf16[128,256]{1,0:T(8,128)(2,1)S(1)} %constant_dynamic-update-slice_fusion.1), channel_id=1, source_target_pairs={{0,1},{1,2},{2,3},{3,4},{4,5},{5,6},{6,7},{7,8},{8,9},{9,10},{10,1... | collective-permute-start | bytes 196616 | tf_op jit(solution)/shard_map/ppermute | solution.py:17
  7.1 4.5 %collective-permute-start.5 = (bf16[128,256]{1,0:T(8,128)(2,1)S(1)}, bf16[128,256]{1,0:T(8,128)(2,1)S(1)}, u32[]{:S(2)}, u32[]{:S(2)}) collective-permute-start(bf16[128,256]{1,0:T(8,128)(2,1)S(1)} %constant_dynamic-update-slice_fusion.1), channel_id=1, source_target_pairs={{0,2},{1,3},{2,4},{3,5},{4,6},{5,7},{6,8},{7,9},{8,10},{9,11},{10,... | collective-permute-start | bytes 196616 | tf_op jit(solution)/shard_map/ppermute | solution.py:17
  11.6 5.8 %collective-permute-start.4 = (bf16[128,256]{1,0:T(8,128)(2,1)S(1)}, bf16[128,256]{1,0:T(8,128)(2,1)S(1)}, u32[]{:S(2)}, u32[]{:S(2)}) collective-permute-start(bf16[128,256]{1,0:T(8,128)(2,1)S(1)} %constant_dynamic-update-slice_fusion.1), channel_id=1, source_target_pairs={{0,3},{1,4},{2,5},{3,6},{4,7},{5,8},{6,9},{7,10},{8,11},{9,12},{10... | collective-permute-start | bytes 196616 | tf_op jit(solution)/shard_map/ppermute | solution.py:17
  17.4 3.8 %collective-permute-start.3 = (bf16[128,256]{1,0:T(8,128)(2,1)S(1)}, bf16[128,256]{1,0:T(8,128)(2,1)S(1)}, u32[]{:S(2)}, u32[]{:S(2)}) collective-permute-start(bf16[128,256]{1,0:T(8,128)(2,1)S(1)} %constant_dynamic-update-slice_fusion.1), channel_id=1, source_target_pairs={{0,4},{1,5},{2,6},{3,7},{4,8},{5,9},{6,10},{7,11},{8,12},{9,13},{1... | collective-permute-start | bytes 196616 | tf_op jit(solution)/shard_map/ppermute | solution.py:17
  21.2 3.3 %collective-permute-start = (bf16[128,256]{1,0:T(8,128)(2,1)S(1)}, bf16[128,256]{1,0:T(8,128)(2,1)S(1)}, u32[]{:S(2)}, u32[]{:S(2)}) collective-permute-start(bf16[128,256]{1,0:T(8,128)(2,1)S(1)} %constant_dynamic-update-slice_fusion.1), channel_id=1, source_target_pairs={{0,7},{1,8},{2,9},{3,10},{4,11},{5,12},{6,13},{7,14},{8,15},{9,16}... | collective-permute-start | bytes 196616 | tf_op jit(solution)/shard_map/ppermute | solution.py:17
  24.6 0.8 dynamic_slice.23
  25.4 6.0 %gather_fusion = s32[1024]{0:T(1024)S(1)} fusion(s32[65536]{0:T(1024)} %param.13, s32[1024]{0:T(1024)S(1)} %broadcast_clamp_fusion), kind=kCustom, calls=%fused_computation | custom fusion | bytes 12288 | tf_op jit(solution)/shard_map/jit(_take)/gather | solution.py:50
  31.5 0.1 reshape.64
  31.6 0.1 reshape.65
  31.8 5.0 %collective-permute-start.1 = (bf16[128,256]{1,0:T(8,128)(2,1)S(1)}, bf16[128,256]{1,0:T(8,128)(2,1)S(1)}, u32[]{:S(2)}, u32[]{:S(2)}) collective-permute-start(bf16[128,256]{1,0:T(8,128)(2,1)S(1)} %constant_dynamic-update-slice_fusion.1), channel_id=1, source_target_pairs={{0,6},{1,7},{2,8},{3,9},{4,10},{5,11},{6,12},{7,13},{8,14},{9,15},... | collective-permute-start | bytes 196616 | tf_op jit(solution)/shard_map/ppermute | solution.py:17
  36.8 2.2 %collective-permute-done.1 = bf16[128,256]{1,0:T(8,128)(2,1)S(1)} collective-permute-done((bf16[128,256]{1,0:T(8,128)(2,1)S(1)}, bf16[128,256]{1,0:T(8,128)(2,1)S(1)}, u32[]{:S(2)}, u32[]{:S(2)}) %collective-permute-start.1) | collective-permute-done | bytes 65568 | tf_op jit(solution)/shard_map/ppermute | solution.py:17
  39.0 10.5 %collective-permute-start.2 = (bf16[128,256]{1,0:T(8,128)(2,1)S(1)}, bf16[128,256]{1,0:T(8,128)(2,1)S(1)}, u32[]{:S(2)}, u32[]{:S(2)}) collective-permute-start(bf16[128,256]{1,0:T(8,128)(2,1)S(1)} %constant_dynamic-update-slice_fusion.1), channel_id=1, source_target_pairs={{0,5},{1,6},{2,7},{3,8},{4,9},{5,10},{6,11},{7,12},{8,13},{9,14},{... | collective-permute-start | bytes 196616 | tf_op jit(solution)/shard_map/ppermute | solution.py:17
  49.5 1.3 collective-permute-done.2
  51.0 7.2 %while.28 = (s32[]{:T(128)}, f32[1024]{0:T(1024)S(1)}, f32[1024]{0:T(1024)S(1)}, f32[1024,128]{1,0:T(8,128)S(1)}, s32[2,512]{1,0:T(2,128)S(1)}, /*index=5*/s32[2...) while((s32[]{:T(128)}, f32[1024]{0:T(1024)S(1)}, ...), condition=%wide.region_3.4_spmd.clone, body=%wide.region_0.0_spmd.clone.sunk | while | flops 945165824 | bytes 8501397 | solution.py:90
  51.1 0.1 broadcast_in_dim.77
  51.1 0.1 eq.55
  51.2 0.1 broadcast_in_dim.78
  51.3 0.1 le.67
  51.5 0.8 fusion.59
  52.3 0.3 fusion.60
  52.6 2.0 %fusion.62 = f32[1024,128]{1,0:T(8,128)S(1)} fusion(f32[1024,512]{0,1:T(8,128)S(1)} %get-tuple-element.416, f32[1024]{0:T(1024)S(1)} %select_maximum_fusion.2, f32[1024,128]{1,0:T(8,128)S(1)} %get-tuple-element.449, f32[1024]{0:T(1024)S(1)} %get-tuple-element.418, pred[]{:T(512)S(6)} %compare.6, bf16[512,256]{1,0:T(8,128)(2,1)S(1)} %dynamic-slice_bitcast_fusion.4), kind=kOutput, calls=%fused_computation.9.clone.1 | convolution fusion | flops 806223872 | bytes 3284993 | tf_op jit(solution)/shard_map/while/body/eval_jaxpr/dot_general | solution.py:80
  54.7 0.1 broadcast_in_dim.77
  54.7 0.1 eq.55
  54.8 0.1 broadcast_in_dim.78
  54.9 0.1 le.67
  55.1 0.8 fusion.59
  55.9 0.3 fusion.60
  56.2 2.0 %fusion.62 = f32[1024,128]{1,0:T(8,128)S(1)} fusion(f32[1024,512]{0,1:T(8,128)S(1)} %get-tuple-element.416, f32[1024]{0:T(1024)S(1)} %select_maximum_fusion.2, f32[1024,128]{1,0:T(8,128)S(1)} %get-tuple-element.449, f32[1024]{0:T(1024)S(1)} %get-tuple-element.418, pred[]{:T(512)S(6)} %compare.6, bf16[512,256]{1,0:T(8,128)(2,1)S(1)} %dynamic-slice_bitcast_fusion.4), kind=kOutput, calls=%fused_computation.9.clone.1 | convolution fusion | flops 806223872 | bytes 3284993 | tf_op jit(solution)/shard_map/while/body/eval_jaxpr/dot_general | solution.py:80
  58.2 0.4 multiply_reduce_fusion
  58.6 9.1 %while.29 = (s32[]{:T(128)}, f32[1024,128]{1,0:T(8,128)S(1)}, f32[2,512,256]{2,1,0:T(8,128)}, s32[2,512]{1,0:T(2,128)S(1)}, s32[2,512]{1,0:T(2,128)S(1)}, /*inde...) while((s32[]{:T(128)}, f32[1024,128]{1,0:T(8,128)S(1)}, ...), condition=%wide.region_6.7_spmd.clone, body=%wide.region_5.6_spmd.clone.sunk | while | flops 678298112 | bytes 16181423 | solution.py:113
  58.7 0.1 broadcast_in_dim.80
  58.7 0.1 eq.59
  58.8 0.1 broadcast_in_dim.81
  58.9 0.1 le.71
  59.0 1.0 fusion.73
  60.1 0.5 fusion.75
  60.5 0.4 fusion.74
  61.0 0.6 convolution_add_fusion.2
  61.6 0.5 fusion.76
  62.1 0.2 copy.17
  62.3 0.8 constant_dynamic-update-slice_fusion.13
  63.3 0.1 eq.59
  63.4 0.1 broadcast_in_dim.81
  63.5 0.1 le.71
  63.6 1.0 fusion.73
  64.6 0.5 fusion.75
  65.1 0.4 fusion.74
  65.5 0.6 convolution_add_fusion.2
  66.1 0.5 fusion.76
  66.7 0.2 copy.17
  66.9 0.8 constant_dynamic-update-slice_fusion.13
  67.7 1.1 slice_bitcast_fusion
  68.8 5.1 %collective-permute-start.7 = (f32[512,256]{1,0:T(8,128)S(1)}, f32[512,256]{1,0:T(8,128)S(1)}, u32[]{:S(2)}, u32[]{:S(2)}) collective-permute-start(f32[512,256]{1,0:T(8,128)S(1)} %slice_bitcast_fusion), channel_id=1, source_target_pairs={{4,0},{5,1},{6,2},{7,3},{8,4},{9,5},{10,6},{11,7},{12,8},{13,9},{1... | collective-permute-start | bytes 1572872 | tf_op jit(solution)/shard_map/ppermute | solution.py:17
  73.9 26.6 %collective-permute-done.7 = f32[512,256]{1,0:T(8,128)S(1)} collective-permute-done((f32[512,256]{1,0:T(8,128)S(1)}, f32[512,256]{1,0:T(8,128)S(1)}, u32[]{:S(2)}, u32[]{:S(2)}) %collective-permute-start.7) | collective-permute-done | bytes 524320 | tf_op jit(solution)/shard_map/ppermute | solution.py:17
  100.5 1.1 bitcast_add_fusion
  101.6 4.9 %collective-permute-start.8 = (f32[256,256]{1,0:T(8,128)S(1)}, f32[256,256]{1,0:T(8,128)S(1)}, u32[]{:S(2)}, u32[]{:S(2)}) collective-permute-start(f32[256,256]{1,0:T(8,128)S(1)} %slice.66), channel_id=1, source_target_pairs={{2,0},{3,1},{4,2},{5,3},{6,4},{7,5},{8,6},{9,7},{10,8},{11,9},{12,... | collective-permute-start | bytes 786440 | tf_op jit(solution)/shard_map/ppermute | solution.py:17
  106.6 10.8 %collective-permute-done.8 = f32[256,256]{1,0:T(8,128)S(1)} collective-permute-done((f32[256,256]{1,0:T(8,128)S(1)}, f32[256,256]{1,0:T(8,128)S(1)}, u32[]{:S(2)}, u32[]{:S(2)}) %collective-permute-start.8) | collective-permute-done | bytes 262176 | tf_op jit(solution)/shard_map/ppermute | solution.py:17
  117.4 6.9 %collective-permute-start.9 = (f32[128,256]{1,0:T(8,128)S(1)}, f32[128,256]{1,0:T(8,128)S(1)}, u32[]{:S(2)}, u32[]{:S(2)}) collective-permute-start(f32[128,256]{1,0:T(8,128)S(1)} %slice.68), channel_id=1, source_target_pairs={{1,0},{2,1},{3,2},{4,3},{5,4},{6,5},{7,6},{8,7},{9,8},{10,9},{11,1... | collective-permute-start | bytes 393224 | tf_op jit(solution)/shard_map/ppermute | solution.py:17
  124.3 0.8 convert_element_type.25
  125.2 0.8 convert_element_type.28
  126.0 3.1 %collective-permute-done.9 = f32[128,256]{1,0:T(8,128)S(1)} collective-permute-done((f32[128,256]{1,0:T(8,128)S(1)}, f32[128,256]{1,0:T(8,128)S(1)}, u32[]{:S(2)}, u32[]{:S(2)}) %collective-permute-start.9) | collective-permute-done | bytes 131104 | tf_op jit(solution)/shard_map/ppermute | solution.py:17
  129.1 0.6 fusion.28
  (58 shorter events, 0.7 us)
Async XLA Ops:
  2.2 48.8 %collective-permute-start.6 = (bf16[128,256]{1,0:T(8,128)(2,1)S(1)}, bf16[128,256]{1,0:T(8,128)(2,1)S(1)}, u32[]{:S(2)}, u32[]{:S(2)}) collective-permute-start(bf16[128,256]{1,0:T(8,128)(2,1)S(1)} %constant_dynamic-update-slice_fusion.1), channel_id=1, source_target_pairs={{0,1},{1,2},{2,3},{3,4},{4,5},{5,6},{6,7},{7,8},{8,9},{9,10},{10,1... | collective-permute-start | bytes 196616 | tf_op jit(solution)/shard_map/ppermute | solution.py:17
  7.1 43.8 %collective-permute-start.5 = (bf16[128,256]{1,0:T(8,128)(2,1)S(1)}, bf16[128,256]{1,0:T(8,128)(2,1)S(1)}, u32[]{:S(2)}, u32[]{:S(2)}) collective-permute-start(bf16[128,256]{1,0:T(8,128)(2,1)S(1)} %constant_dynamic-update-slice_fusion.1), channel_id=1, source_target_pairs={{0,2},{1,3},{2,4},{3,5},{4,6},{5,7},{6,8},{7,9},{8,10},{9,11},{10,... | collective-permute-start | bytes 196616 | tf_op jit(solution)/shard_map/ppermute | solution.py:17
  11.6 39.3 %collective-permute-start.4 = (bf16[128,256]{1,0:T(8,128)(2,1)S(1)}, bf16[128,256]{1,0:T(8,128)(2,1)S(1)}, u32[]{:S(2)}, u32[]{:S(2)}) collective-permute-start(bf16[128,256]{1,0:T(8,128)(2,1)S(1)} %constant_dynamic-update-slice_fusion.1), channel_id=1, source_target_pairs={{0,3},{1,4},{2,5},{3,6},{4,7},{5,8},{6,9},{7,10},{8,11},{9,12},{10... | collective-permute-start | bytes 196616 | tf_op jit(solution)/shard_map/ppermute | solution.py:17
  17.4 33.5 %collective-permute-start.3 = (bf16[128,256]{1,0:T(8,128)(2,1)S(1)}, bf16[128,256]{1,0:T(8,128)(2,1)S(1)}, u32[]{:S(2)}, u32[]{:S(2)}) collective-permute-start(bf16[128,256]{1,0:T(8,128)(2,1)S(1)} %constant_dynamic-update-slice_fusion.1), channel_id=1, source_target_pairs={{0,4},{1,5},{2,6},{3,7},{4,8},{5,9},{6,10},{7,11},{8,12},{9,13},{1... | collective-permute-start | bytes 196616 | tf_op jit(solution)/shard_map/ppermute | solution.py:17
  21.2 10.5 %collective-permute-start = (bf16[128,256]{1,0:T(8,128)(2,1)S(1)}, bf16[128,256]{1,0:T(8,128)(2,1)S(1)}, u32[]{:S(2)}, u32[]{:S(2)}) collective-permute-start(bf16[128,256]{1,0:T(8,128)(2,1)S(1)} %constant_dynamic-update-slice_fusion.1), channel_id=1, source_target_pairs={{0,7},{1,8},{2,9},{3,10},{4,11},{5,12},{6,13},{7,14},{8,15},{9,16}... | collective-permute-start | bytes 196616 | tf_op jit(solution)/shard_map/ppermute | solution.py:17
  25.4 6.1 %copy-start = (bf16[128,1024]{1,0:T(8,128)(2,1)S(1)}, bf16[128,1024]{1,0:T(8,128)(2,1)}, u32[]{:S(2)}) copy-start(bf16[128,1024]{1,0:T(8,128)(2,1)} %param.9) | copy-start | bytes 786436
  25.4 6.2 %copy-start.1 = (bf16[128,1024]{1,0:T(8,128)(2,1)S(1)}, bf16[128,1024]{1,0:T(8,128)(2,1)}, u32[]{:S(2)}) copy-start(bf16[128,1024]{1,0:T(8,128)(2,1)} %param.12) | copy-start | bytes 786436
  25.4 25.5 %copy-start.2 = (bf16[128,128]{1,0:T(8,128)(2,1)S(1)}, bf16[128,128]{1,0:T(8,128)(2,1)}, u32[]{:S(2)}) copy-start(bf16[128,128]{1,0:T(8,128)(2,1)} %param.10) | copy-start | bytes 98308
  25.4 25.6 %copy-start.3 = (bf16[128,128]{1,0:T(8,128)(2,1)S(1)}, bf16[128,128]{1,0:T(8,128)(2,1)}, u32[]{:S(2)}) copy-start(bf16[128,128]{1,0:T(8,128)(2,1)} %param.11) | copy-start | bytes 98308
  31.8 7.2 %collective-permute-start.1 = (bf16[128,256]{1,0:T(8,128)(2,1)S(1)}, bf16[128,256]{1,0:T(8,128)(2,1)S(1)}, u32[]{:S(2)}, u32[]{:S(2)}) collective-permute-start(bf16[128,256]{1,0:T(8,128)(2,1)S(1)} %constant_dynamic-update-slice_fusion.1), channel_id=1, source_target_pairs={{0,6},{1,7},{2,8},{3,9},{4,10},{5,11},{6,12},{7,13},{8,14},{9,15},... | collective-permute-start | bytes 196616 | tf_op jit(solution)/shard_map/ppermute | solution.py:17
  39.0 11.8 %collective-permute-start.2 = (bf16[128,256]{1,0:T(8,128)(2,1)S(1)}, bf16[128,256]{1,0:T(8,128)(2,1)S(1)}, u32[]{:S(2)}, u32[]{:S(2)}) collective-permute-start(bf16[128,256]{1,0:T(8,128)(2,1)S(1)} %constant_dynamic-update-slice_fusion.1), channel_id=1, source_target_pairs={{0,5},{1,6},{2,7},{3,8},{4,9},{5,10},{6,11},{7,12},{8,13},{9,14},{... | collective-permute-start | bytes 196616 | tf_op jit(solution)/shard_map/ppermute | solution.py:17
  68.8 31.7 %collective-permute-start.7 = (f32[512,256]{1,0:T(8,128)S(1)}, f32[512,256]{1,0:T(8,128)S(1)}, u32[]{:S(2)}, u32[]{:S(2)}) collective-permute-start(f32[512,256]{1,0:T(8,128)S(1)} %slice_bitcast_fusion), channel_id=1, source_target_pairs={{4,0},{5,1},{6,2},{7,3},{8,4},{9,5},{10,6},{11,7},{12,8},{13,9},{1... | collective-permute-start | bytes 1572872 | tf_op jit(solution)/shard_map/ppermute | solution.py:17
  101.6 15.7 %collective-permute-start.8 = (f32[256,256]{1,0:T(8,128)S(1)}, f32[256,256]{1,0:T(8,128)S(1)}, u32[]{:S(2)}, u32[]{:S(2)}) collective-permute-start(f32[256,256]{1,0:T(8,128)S(1)} %slice.66), channel_id=1, source_target_pairs={{2,0},{3,1},{4,2},{5,3},{6,4},{7,5},{8,6},{9,7},{10,8},{11,9},{12,... | collective-permute-start | bytes 786440 | tf_op jit(solution)/shard_map/ppermute | solution.py:17
  117.4 11.7 %collective-permute-start.9 = (f32[128,256]{1,0:T(8,128)S(1)}, f32[128,256]{1,0:T(8,128)S(1)}, u32[]{:S(2)}, u32[]{:S(2)}) collective-permute-start(f32[128,256]{1,0:T(8,128)S(1)} %slice.68), channel_id=1, source_target_pairs={{1,0},{2,1},{3,2},{4,3},{5,4},{6,5},{7,6},{8,7},{9,8},{10,9},{11,1... | collective-permute-start | bytes 393224 | tf_op jit(solution)/shard_map/ppermute | solution.py:17
where the time goes:
time: 130 us
  starting transfers between devices  54.8 us (42%)
  waiting for transfers between devices  44 us (34%)
  local copies, waits for them, and re-layouts  15.6 us (12%)
  matrix products  11.5 us (9%)
  other arithmetic  2.49 us (2%)
    ppermute x10, starting transfers between devices, from_behind(): return lax.ppermute(block, axis, route)  54.8 us
    ppermute x10, waiting for transfers between devices, from_behind(): return lax.ppermute(block, axis, route)  44 us
    gather x2, local copies, waits for them, and re-layouts, body(): key_doc = jnp.take(doc_ids, jnp.clip(key_pos, 0, doc_ids.shape[0] - 1))  6.05 us
    dot_general x6, matrix products, contract_last(): lax.dot_general(left_op, right_op, (((1,), (1,)), ((), ())), preferred_el...  4.52 us
    dot_general x2, matrix products, forward_tile(): jnp.dot(weights, kv_blk[:, head_width:].astype(jnp.float32), precision=la...  3.91 us
  transfers between devices with their start and end apart: 10, of which 5 were waited for; matrix products, arithmetic and copies ran while one was open for 7% of the time, Pallas kernels for 0%

commit v1 on v0

v1 whole, which is shorter than its diff:
```python
import math

import jax
import jax.numpy as jnp
from jax import lax
from jax.experimental import pallas as pl
from jax.experimental.pallas import tpu as pltpu
from jax.sharding import PartitionSpec as P

REACH = 8
HEADS = 8
MASKED = -1e30


def contract_last(left_op, right_op):
    return lax.dot_general(
        left_op, right_op, (((1,), (1,)), ((), ())), preferred_element_type=jnp.float32
    )


def contract_first(left_op, right_op):
    return lax.dot_general(
        left_op, right_op, (((0,), (0,)), ((), ())), preferred_element_type=jnp.float32
    )


def attention_kernel(me_ref, kv_ref, q_ref, g_ref, doc_ref, out_ref, dq_ref, send_ref, bias_ref, dk_ref, dv_ref):
    tokens, width = kv_ref.shape[1], kv_ref.shape[2] // 2
    span = REACH * tokens
    scale = 1.0 / math.sqrt(width)
    me = me_ref[0]
    mine = lax.rem(me, REACH)
    row = me - mine

    query_doc = jnp.broadcast_to(doc_ref[pl.ds(me, 1), :], (tokens, tokens)).T
    lane = lax.broadcasted_iota(jnp.int32, (tokens, tokens), 1)
    line = lax.broadcasted_iota(jnp.int32, (tokens, tokens), 0)
    for j in range(REACH):
        block = jnp.where(j <= mine, row + j, row - REACH + j)
        key_doc = doc_ref[pl.ds(jnp.maximum(block, 0), 1), :]
        reach = jnp.where(block < 0, -1, jnp.where(j == mine, 0, tokens))
        visible = (key_doc == query_doc) & (lane <= line + reach) & (reach >= 0)
        bias_ref[:, j * tokens : (j + 1) * tokens] = jnp.where(visible, 0.0, MASKED)

    keys = kv_ref[:, :, :width].reshape(span, width)
    values = kv_ref[:, :, width:].reshape(span, width)
    values_one = jnp.concatenate([values, jnp.ones_like(values)], axis=1)

    for h in range(HEADS):
        cols = slice(h * width, (h + 1) * width)
        query = q_ref[:, cols]
        scores = contract_last(query, keys) * (scale * math.log2(math.e)) + bias_ref[...]
        top = jnp.max(scores, axis=1, keepdims=True)
        weights = jnp.exp2(scores - top).astype(jnp.bfloat16)
        sums = jnp.dot(weights, values_one, preferred_element_type=jnp.float32)
        inverse = 1.0 / sums[:, width:]
        output = sums[:, :width] * inverse
        out_ref[:, cols] = output.astype(jnp.bfloat16)
        grad = (g_ref[:, cols].astype(jnp.float32) * (inverse * scale)).astype(jnp.bfloat16)
        delta = jnp.sum(grad.astype(jnp.float32) * output, axis=1, keepdims=True)
        slope = contract_last(grad, values) - delta
        score_grad = (weights.astype(jnp.float32) * slope).astype(jnp.bfloat16)
        dq_ref[:, cols] = jnp.dot(score_grad, keys, preferred_element_type=jnp.float32).astype(jnp.bfloat16)
        dk = contract_first(query, score_grad)
        dv = contract_first(grad, weights)
        if h == 0:
            dk_ref[...] = dk
            dv_ref[...] = dv
        else:
            dk_ref[...] += dk
            dv_ref[...] += dv

    for j in range(REACH):
        at = slice(j * tokens, (j + 1) * tokens)
        send_ref[j, :, :width] = dk_ref[:, at].T.astype(jnp.bfloat16)
        send_ref[j, :, width:] = (dv_ref[:, at].T * (1.0 / scale)).astype(jnp.bfloat16)


def attention(me, window, queries, d_out, docs):
    tokens, wide = queries.shape
    span = window.shape[0] * tokens
    width = window.shape[2] // 2
    vmem = pl.BlockSpec(memory_space=pltpu.VMEM)
    return pl.pallas_call(
        attention_kernel,
        out_shape=(
            jax.ShapeDtypeStruct((tokens, wide), jnp.bfloat16),
            jax.ShapeDtypeStruct((tokens, wide), jnp.bfloat16),
            jax.ShapeDtypeStruct(window.shape, jnp.bfloat16),
        ),
        in_specs=[pl.BlockSpec(memory_space=pltpu.SMEM), vmem, vmem, vmem, vmem],
        out_specs=(vmem, vmem, vmem),
        scratch_shapes=[
            pltpu.VMEM((tokens, span), jnp.float32),
            pltpu.VMEM((width, span), jnp.float32),
            pltpu.VMEM((width, span), jnp.float32),
        ],
        compiler_params=pltpu.CompilerParams(vmem_limit_bytes=40 * 1024 * 1024),
        cost_estimate=pl.CostEstimate(
            flops=12 * HEADS * tokens * span * width, bytes_accessed=3 * 1024 * 1024, transcendentals=HEADS * tokens * span
        ),
    )(me, window, queries, d_out, docs)


def body(queries, keys, values, d_out, doc_ids):
    axes = ("outer", "inner")
    n_inner = lax.axis_size("inner")
    total = lax.axis_size("outer") * n_inner
    me = lax.axis_index("outer") * n_inner + lax.axis_index("inner")
    mine = lax.rem(me, REACH)
    tokens, width = keys.shape
    lines = [[start + k for k in range(REACH)] for start in range(0, n_inner, REACH)]
    slot = jnp.arange(REACH, dtype=jnp.int32)[:, None, None]

    def exchange(parts):
        return lax.all_to_all(parts, "inner", 0, 0, axis_index_groups=lines)

    packed = jnp.concatenate([keys, values], axis=1)
    behind = lax.ppermute(packed, axes, [(i, i + REACH) for i in range(total - REACH)])
    window = exchange(jnp.where(slot >= mine, packed[None], behind[None]))
    attended, grad_queries, parts = attention(
        me.reshape(1), window, queries, d_out, doc_ids.reshape(-1, tokens)
    )
    terms = exchange(parts).astype(jnp.float32)
    passed = jnp.sum(jnp.where(slot < mine, terms, 0.0), axis=0).astype(jnp.bfloat16)
    passed = lax.ppermute(passed, axes, [(i, i - REACH) for i in range(REACH, total)])
    owned = jnp.sum(jnp.where(slot >= mine, terms, 0.0), axis=0) + passed.astype(jnp.float32)
    grad_keys = owned[:, :width].astype(jnp.bfloat16)
    grad_values = owned[:, width:].astype(jnp.bfloat16)
    return (attended, grad_queries, grad_keys, grad_values)


def solution(mesh):
    split = P(("outer", "inner"), None)
    return jax.shard_map(
        body,
        mesh=mesh,
        in_specs=(split, split, split, split, P()),
        out_specs=(split, split, split, split),
        check_vma=False,
    )
```

time: 130 us -> 73.1 us (0.56)
  the two profiles are of different devices: /device:TPU:255 before, /device:TPU:199 now
where the time goes in v1:
time: 73.1 us; the launch traced here: 72.8 us
  waiting for transfers between devices  26.1 us (36%)
  blocking collectives  24.8 us (34%)
  starting transfers between devices  11.1 us (15%)
  Pallas kernels  8.16 us (11%)
  local copies, waits for them, and re-layouts  1.44 us (2%)
    all_to_all x1, blocking collectives, exchange(): return lax.all_to_all(parts, 'inner', 0, 0, axis_index_groups=lines)  24.8 us
    all_to_all x1, waiting for transfers between devices, exchange(): return lax.all_to_all(parts, 'inner', 0, 0, axis_index_groups=lines)  17.9 us
    pallas_call x1, Pallas kernels, attention(): pl.pallas_call(attention_kernel, out_shape=(jax.ShapeDtypeStruct((tokens,...  8.16 us
    ppermute x1, waiting for transfers between devices, body(): lax.ppermute(passed, axes, [(i, i - REACH) for i in range(REACH, total)])  6.98 us
    ppermute x1, starting transfers between devices, body(): lax.ppermute(packed, axes, [(i, i + REACH) for i in range(total - REACH)])  5.69 us
    all_to_all x1, starting transfers between devices, exchange(): return lax.all_to_all(parts, 'inner', 0, 0, axis_index_groups=lines)  3.49 us
    ppermute x1, starting transfers between devices, body(): lax.ppermute(passed, axes, [(i, i - REACH) for i in range(REACH, total)])  1.92 us
  transfers between devices with their start and end apart: 3, of which 3 were waited for; matrix products, arithmetic and copies ran while one was open for 0% of the time, Pallas kernels for 0%

profile of v1, /device:TPU:199, one launch (start us, length us, event | category | flops | bytes accessed | tf_op | source)
XLA Modules:
  0.0 72.8 jit_solution(5602815775202898069)
XLA Ops:
  0.6 0.0 copy-start.3
  0.6 0.8 %constant_dynamic-update-slice_fusion.1 = bf16[128,256]{1,0:T(8,128)(2,1)S(1)} fusion(bf16[128,128]{1,0:T(8,128)(2,1)} %param.6), kind=kLoop, calls=%fused_computation.7 | loop fusion | bytes 65536
  1.4 0.0 copy-done.3
  1.4 5.7 %collective-permute-start = (bf16[128,256]{1,0:T(8,128)(2,1)S(1)}, bf16[128,256]{1,0:T(8,128)(2,1)S(1)}, u32[]{:S(2)}, u32[]{:S(2)}) collective-permute-start(bf16[128,256]{1,0:T(8,128)(2,1)S(1)} %constant_dynamic-update-slice_fusion), channel_id=1, source_target_pairs={{0,8},{1,9},{2,10},{3,11},{4,12},{5,13},{6,14},{7,15},{8,16},{9,17... | collective-permute-start | bytes 196616 | tf_op jit(solution)/shard_map/ppermute | solution.py:119
  7.1 1.3 %collective-permute-done = bf16[128,256]{1,0:T(8,128)(2,1)S(1)} collective-permute-done((bf16[128,256]{1,0:T(8,128)(2,1)S(1)}, bf16[128,256]{1,0:T(8,128)(2,1)S(1)}, u32[]{:S(2)}, u32[]{:S(2)}) %collective-permute-start) | collective-permute-done | bytes 65568 | tf_op jit(solution)/shard_map/ppermute | solution.py:119
  8.4 0.1 broadcast_select_fusion
  8.5 0.0 copy-start
  8.6 0.0 copy-start.1
  8.6 0.0 copy-start.2
  8.6 24.8 %all_to_all.10.kv_ref = bf16[8,128,256]{2,1,0:T(8,128)(2,1)S(1)} all-to-all(bf16[8,128,256]{2,1,0:T(8,128)(2,1)S(1)} %broadcast_select_fusion), channel_id=1, replica_groups={{0,1,2,3,4,5,6,7},{8,9,10,11,12,13,14,15},{16,17,18,19,20,21,22,23},{24..., dimensions={0} | all-to-all | bytes 1048576 | tf_op jit(solution)/shard_map/all_to_all | solution.py:116
  33.4 0.0 copy-done
  33.4 0.0 copy-done.1
  33.4 0.0 copy-done.2
  33.4 8.2 %shard_map.84 = (bf16[128,1024]{1,0:T(8,128)(2,1)}, bf16[128,1024]{1,0:T(8,128)(2,1)}, bf16[8,128,256]{2,1,0:T(8,128)(2,1)}) custom-call(s32[1]{0:T(128)} %bitcast.me_ref, bf16[8,128,256]{2,1,0:T(8,128)(2,1)S(1)} %all_to_all.10.kv_ref, bf16[128,1024]{1,0:T(8,128)(2,1)S(1)} %copy-done, bf16[128,1024]{1,0:T(8,128)(2,1)S(1)} %copy-done.1, s32[512,128]{1,0:T(8,128)S(1)} %bitcast.2), custom_call_target="tpu_custom_call" | custom-call | flops 1610612736 | bytes 3145728 | tf_op jit(solution)/shard_map/pallas_call | solution.py:84
  41.5 3.5 %all-to-all-start.1 = ((bf16[8,128,256]{2,1,0:T(8,128)(2,1)}), bf16[8,128,256]{2,1,0:T(8,128)(2,1)S(1)}, u32[]{:S(2)}, u32[]{:S(2)}) async-start(bf16[8,128,256]{2,1,0:T(8,128)(2,1)} %get-tuple-element.9), calls=%async_computation.1 | async-start | bytes 1048576 | tf_op jit(solution)/shard_map/all_to_all | solution.py:116
  45.1 17.9 %all-to-all-done.1 = bf16[8,128,256]{2,1,0:T(8,128)(2,1)S(1)} async-done(((bf16[8,128,256]{2,1,0:T(8,128)(2,1)}), bf16[8,128,256]{2,1,0:T(8,128)(2,1)S(1)}, u32[]{:S(2)}, u32[]{:S(2)}) %all-to-all-start.1) | async-done | bytes 524320 | tf_op jit(solution)/shard_map/all_to_all | solution.py:116
  62.9 0.3 fusion.1
  63.2 1.9 %collective-permute-start.1 = (bf16[128,256]{1,0:T(8,128)(2,1)S(1)}, bf16[128,256]{1,0:T(8,128)(2,1)S(1)}, u32[]{:S(2)}, u32[]{:S(2)}) collective-permute-start(bf16[128,256]{1,0:T(8,128)(2,1)S(1)} %get-tuple-element.10), channel_id=1, source_target_pairs={{8,0},{9,1},{10,2},{11,3},{12,4},{13,5},{14,6},{15,7},{16,8},{17,9... | collective-permute-start | bytes 196616 | tf_op jit(solution)/shard_map/ppermute | solution.py:126
  65.1 7.0 %collective-permute-done.1 = bf16[128,256]{1,0:T(8,128)(2,1)S(1)} collective-permute-done((bf16[128,256]{1,0:T(8,128)(2,1)S(1)}, bf16[128,256]{1,0:T(8,128)(2,1)S(1)}, u32[]{:S(2)}, u32[]{:S(2)}) %collective-permute-start.1) | collective-permute-done | bytes 65568 | tf_op jit(solution)/shard_map/ppermute | solution.py:126
  72.1 0.6 fusion.2
  (4 shorter events, 0.0 us)
Async XLA Ops:
  0.6 0.8 %copy-start.3 = (bf16[128,128]{1,0:T(8,128)(2,1)S(1)}, bf16[128,128]{1,0:T(8,128)(2,1)}, u32[]{:S(2)}) copy-start(bf16[128,128]{1,0:T(8,128)(2,1)} %param.7) | copy-start | bytes 98308
  1.4 7.0 %collective-permute-start = (bf16[128,256]{1,0:T(8,128)(2,1)S(1)}, bf16[128,256]{1,0:T(8,128)(2,1)S(1)}, u32[]{:S(2)}, u32[]{:S(2)}) collective-permute-start(bf16[128,256]{1,0:T(8,128)(2,1)S(1)} %constant_dynamic-update-slice_fusion), channel_id=1, source_target_pairs={{0,8},{1,9},{2,10},{3,11},{4,12},{5,13},{6,14},{7,15},{8,16},{9,17... | collective-permute-start | bytes 196616 | tf_op jit(solution)/shard_map/ppermute | solution.py:119
  8.5 24.8 %copy-start = (bf16[128,1024]{1,0:T(8,128)(2,1)S(1)}, bf16[128,1024]{1,0:T(8,128)(2,1)}, u32[]{:S(2)}) copy-start(bf16[128,1024]{1,0:T(8,128)(2,1)} %q_ref.1) | copy-start | bytes 786436
  8.6 24.8 %copy-start.1 = (bf16[128,1024]{1,0:T(8,128)(2,1)S(1)}, bf16[128,1024]{1,0:T(8,128)(2,1)}, u32[]{:S(2)}) copy-start(bf16[128,1024]{1,0:T(8,128)(2,1)} %g_ref.1) | copy-start | bytes 786436
  8.6 24.8 %copy-start.2 = (s32[65536]{0:T(1024)S(1)}, s32[65536]{0:T(1024)}, u32[]{:S(2)}) copy-start(s32[65536]{0:T(1024)} %param.9) | copy-start | bytes 786436
  41.5 21.4 %all-to-all-start.1 = ((bf16[8,128,256]{2,1,0:T(8,128)(2,1)}), bf16[8,128,256]{2,1,0:T(8,128)(2,1)S(1)}, u32[]{:S(2)}, u32[]{:S(2)}) async-start(bf16[8,128,256]{2,1,0:T(8,128)(2,1)} %get-tuple-element.9), calls=%async_computation.1 | async-start | bytes 1048576 | tf_op jit(solution)/shard_map/all_to_all | solution.py:116
  63.2 8.9 %collective-permute-start.1 = (bf16[128,256]{1,0:T(8,128)(2,1)S(1)}, bf16[128,256]{1,0:T(8,128)(2,1)S(1)}, u32[]{:S(2)}, u32[]{:S(2)}) collective-permute-start(bf16[128,256]{1,0:T(8,128)(2,1)S(1)} %get-tuple-element.10), channel_id=1, source_target_pairs={{8,0},{9,1},{10,2},{11,3},{12,4},{13,5},{14,6},{15,7},{16,8},{17,9... | collective-permute-start | bytes 196616 | tf_op jit(solution)/shard_map/ppermute | solution.py:126

commit v2 on v1

v2 whole, which is shorter than its diff:
```python
import math

import jax
import jax.numpy as jnp
from jax import lax
from jax.experimental import pallas as pl
from jax.experimental.pallas import tpu as pltpu
from jax.sharding import PartitionSpec as P

REACH = 8
HEADS = 8
MASKED = -1e30
GATHER_ORDER = (5, 6, 7, 0, 1, 2, 3, 4)
RETURN_ORDER = (5, 6, 7, 0, 1, 2, 3, 4)


def contract_last(left_op, right_op):
    return lax.dot_general(
        left_op, right_op, (((1,), (1,)), ((), ())), preferred_element_type=jnp.float32
    )


def contract_first(left_op, right_op):
    return lax.dot_general(
        left_op, right_op, (((0,), (0,)), ((), ())), preferred_element_type=jnp.float32
    )


def pack_kernel(key_ref, value_ref, out_ref):
    width = key_ref.shape[1]
    out_ref[:, :width] = key_ref[...]
    out_ref[:, width:] = value_ref[...]


def attention_kernel(
    me_ref, kv_ref, q_ref, g_ref, doc_ref, out_ref, dq_ref, send_ref,
    bias_ref, w_ref, ds_ref, rows_ref, grads_ref,
):
    tokens, width = kv_ref.shape[1], kv_ref.shape[2] // 2
    span = REACH * tokens
    scale = 1.0 / math.sqrt(width)
    me = me_ref[0]
    mine = lax.rem(me, REACH)
    row = me - mine

    query_doc = jnp.broadcast_to(doc_ref[pl.ds(me, 1), :], (tokens, tokens)).T
    lane = lax.broadcasted_iota(jnp.int32, (tokens, tokens), 1)
    line = lax.broadcasted_iota(jnp.int32, (tokens, tokens), 0)
    for k, j in enumerate(GATHER_ORDER):
        block = jnp.where(j <= mine, row + j, row - REACH + j)
        key_doc = doc_ref[pl.ds(jnp.maximum(block, 0), 1), :]
        reach = jnp.where(block < 0, -tokens, jnp.where(j == mine, 0, tokens))
        visible = (key_doc == query_doc) & (lane <= line + reach)
        bias_ref[:, k * tokens : (k + 1) * tokens] = jnp.where(visible, 0.0, MASKED)

    keys = kv_ref[:, :, :width].reshape(span, width)
    values = kv_ref[:, :, width:].reshape(span, width)
    values_one = jnp.concatenate([values, jnp.ones_like(values)], axis=1)

    heads = [
        (slice(h * width, (h + 1) * width), slice(h * tokens, (h + 1) * tokens)) for h in range(HEADS)
    ]
    for cols, rows in heads:
        query = q_ref[:, cols]
        rows_ref[rows, :] = query
        scores = contract_last(query, keys) * (scale * math.log2(math.e)) + bias_ref[...]
        top = jnp.max(scores, axis=1, keepdims=True)
        w_ref[rows, :] = jnp.exp2(scores - top).astype(jnp.bfloat16)
    sums_all = jnp.dot(w_ref[...], values_one, preferred_element_type=jnp.float32)
    deltas = []
    for cols, rows in heads:
        inverse = 1.0 / sums_all[rows, width:]
        output = sums_all[rows, :width] * inverse
        out_ref[:, cols] = output.astype(jnp.bfloat16)
        grad = (g_ref[:, cols].astype(jnp.float32) * (inverse * scale)).astype(jnp.bfloat16)
        grads_ref[rows, :] = grad
        deltas.append(jnp.sum(grad.astype(jnp.float32) * output, axis=1, keepdims=True))
    for (cols, rows), delta in zip(heads, deltas):
        slope = contract_last(grads_ref[rows, :], values) - delta
        ds_ref[rows, :] = (w_ref[rows, :].astype(jnp.float32) * slope).astype(jnp.bfloat16)
    dq = jnp.dot(ds_ref[...], keys, preferred_element_type=jnp.float32).astype(jnp.bfloat16)
    for cols, rows in heads:
        dq_ref[:, cols] = dq[rows, :]
    dk = contract_first(rows_ref[...], ds_ref[...])
    dv = contract_first(grads_ref[...], w_ref[...])
    for k, j in enumerate(GATHER_ORDER):
        at = slice(k * tokens, (k + 1) * tokens)
        send_ref[RETURN_ORDER.index(j), :, :width] = dk[:, at].T.astype(jnp.bfloat16)
        send_ref[RETURN_ORDER.index(j), :, width:] = (dv[:, at].T * (1.0 / scale)).astype(jnp.bfloat16)


def attention(me, window, queries, d_out, docs):
    tokens, wide = queries.shape
    span = window.shape[0] * tokens
    width = window.shape[2] // 2
    vmem = pl.BlockSpec(memory_space=pltpu.VMEM)
    return pl.pallas_call(
        attention_kernel,
        out_shape=(
            jax.ShapeDtypeStruct((tokens, wide), jnp.bfloat16),
            jax.ShapeDtypeStruct((tokens, wide), jnp.bfloat16),
            jax.ShapeDtypeStruct(window.shape, jnp.bfloat16),
        ),
        in_specs=[pl.BlockSpec(memory_space=pltpu.SMEM), vmem, vmem, vmem, vmem],
        out_specs=(vmem, vmem, vmem),
        scratch_shapes=[
            pltpu.VMEM((tokens, span), jnp.float32),
            pltpu.VMEM((HEADS * tokens, span), jnp.bfloat16),
            pltpu.VMEM((HEADS * tokens, span), jnp.bfloat16),
            pltpu.VMEM((HEADS * tokens, width), jnp.bfloat16),
            pltpu.VMEM((HEADS * tokens, width), jnp.bfloat16),
        ],
        compiler_params=pltpu.CompilerParams(vmem_limit_bytes=40 * 1024 * 1024),
        cost_estimate=pl.CostEstimate(
            flops=12 * HEADS * tokens * span * width,
            bytes_accessed=3 * 1024 * 1024,
            transcendentals=HEADS * tokens * span,
        ),
    )(me, window, queries, d_out, docs)


def body(queries, keys, values, d_out, doc_ids):
    axes = ("outer", "inner")
    n_inner = lax.axis_size("inner")
    total = lax.axis_size("outer") * n_inner
    me = lax.axis_index("outer") * n_inner + lax.axis_index("inner")
    mine = lax.rem(me, REACH)
    tokens, width = keys.shape

    def exchange(parts, order):
        lines = [[start + k for k in order] for start in range(0, n_inner, REACH)]
        return lax.all_to_all(parts, "inner", 0, 0, axis_index_groups=lines)

    def partner(order):
        return jnp.array(order, dtype=jnp.int32)[:, None, None]

    packed = jnp.concatenate([keys, values], axis=1)
    behind = lax.ppermute(packed, axes, [(i, i + REACH) for i in range(total - REACH)])
    outgoing = jnp.where(partner(GATHER_ORDER) >= mine, packed[None], behind[None])
    window = exchange(outgoing, GATHER_ORDER)
    attended, grad_queries, parts = attention(
        me.reshape(1), window, queries, d_out, doc_ids.reshape(-1, tokens)
    )
    terms = exchange(parts, RETURN_ORDER).astype(jnp.float32)
    ahead = partner(RETURN_ORDER) < mine
    passed = jnp.sum(jnp.where(ahead, terms, 0.0), axis=0).astype(jnp.bfloat16)
    passed = lax.ppermute(passed, axes, [(i, i - REACH) for i in range(REACH, total)])
    owned = jnp.sum(jnp.where(ahead, 0.0, terms), axis=0) + passed.astype(jnp.float32)
    grad_keys = owned[:, :width].astype(jnp.bfloat16)
    grad_values = owned[:, width:].astype(jnp.bfloat16)
    return (attended, grad_queries, grad_keys, grad_values)


def solution(mesh):
    split = P(("outer", "inner"), None)
    return jax.shard_map(
        body,
        mesh=mesh,
        in_specs=(split, split, split, split, P()),
        out_specs=(split, split, split, split),
        check_vma=False,
    )
```

time: 73.1 us -> 62.6 us (0.86)
  the two profiles are of different devices: /device:TPU:199 before, /device:TPU:215 now
where the time goes in v2:
time: 62.6 us; the launch traced here: 62.3 us
  blocking collectives  39.3 us (63%)
  starting transfers between devices  7.61 us (12%)
  waiting for transfers between devices  7.61 us (12%)
  Pallas kernels  4.64 us (7%)
  local copies, waits for them, and re-layouts  2.09 us (3%)
  between operations  0.72 us (1%)
    all_to_all x2, blocking collectives, exchange(): return lax.all_to_all(parts, 'inner', 0, 0, axis_index_groups=lines)  39.3 us
    ppermute x1, waiting for transfers between devices, body(): lax.ppermute(passed, axes, [(i, i - REACH) for i in range(REACH, total)])  6.98 us
    ppermute x1, starting transfers between devices, body(): lax.ppermute(packed, axes, [(i, i + REACH) for i in range(total - REACH)])  5.69 us
    pallas_call x1, Pallas kernels, attention(): pl.pallas_call(attention_kernel, out_shape=(jax.ShapeDtypeStruct((tokens,...  4.64 us
    ppermute x1, starting transfers between devices, body(): lax.ppermute(passed, axes, [(i, i - REACH) for i in range(REACH, total)])  1.92 us
    unnamed x11, local copies, waits for them, and re-layouts  1.44 us
  transfers between devices with their start and end apart: 2, of which 2 were waited for; matrix products, arithmetic and copies ran while one was open for 0% of the time, Pallas kernels for 0%

profile of v2, /device:TPU:215, one launch (start us, length us, event | category | flops | bytes accessed | tf_op | source)
XLA Modules:
  0.0 62.3 jit_solution(15305889730845367194)
XLA Ops:
  0.6 0.0 copy-start.3
  0.6 0.8 %constant_dynamic-update-slice_fusion.1 = bf16[128,256]{1,0:T(8,128)(2,1)S(1)} fusion(bf16[128,128]{1,0:T(8,128)(2,1)} %param.8), kind=kLoop, calls=%fused_computation.7 | loop fusion | bytes 65536
  1.4 0.0 copy-done.3
  1.4 5.7 %collective-permute-start = (bf16[128,256]{1,0:T(8,128)(2,1)S(1)}, bf16[128,256]{1,0:T(8,128)(2,1)S(1)}, u32[]{:S(2)}, u32[]{:S(2)}) collective-permute-start(bf16[128,256]{1,0:T(8,128)(2,1)S(1)} %constant_dynamic-update-slice_fusion), channel_id=1, source_target_pairs={{0,8},{1,9},{2,10},{3,11},{4,12},{5,13},{6,14},{7,15},{8,16},{9,17... | collective-permute-start | bytes 196616 | tf_op jit(solution)/shard_map/ppermute | solution.py:138
  7.1 0.0 copy-start.4
  7.1 0.6 %copy-done.4 = s32[8]{0:T(128)S(1)} copy-done((s32[8]{0:T(128)S(1)}, s32[8]{0:T(128)}, u32[]{:S(2)}) %copy-start.4) | copy-done | bytes 56
  7.8 0.6 %collective-permute-done = bf16[128,256]{1,0:T(8,128)(2,1)S(1)} collective-permute-done((bf16[128,256]{1,0:T(8,128)(2,1)S(1)}, bf16[128,256]{1,0:T(8,128)(2,1)S(1)}, u32[]{:S(2)}, u32[]{:S(2)}) %collective-permute-start) | collective-permute-done | bytes 65568 | tf_op jit(solution)/shard_map/ppermute | solution.py:138
  8.4 0.1 broadcast_select_fusion
  8.6 0.0 copy-start
  8.6 0.0 copy-start.1
  8.6 0.0 copy-start.2
  8.6 19.5 %all_to_all.10.kv_ref = bf16[8,128,256]{2,1,0:T(8,128)(2,1)S(1)} all-to-all(bf16[8,128,256]{2,1,0:T(8,128)(2,1)S(1)} %broadcast_select_fusion), channel_id=1, replica_groups={{5,6,7,0,1,2,3,4},{13,14,15,8,9,10,11,12},{21,22,23,16,17,18,19,20},{29..., dimensions={0} | all-to-all | bytes 1048576 | tf_op jit(solution)/shard_map/all_to_all | solution.py:132
  28.1 0.0 copy-done
  28.1 0.0 copy-done.1
  28.1 0.0 copy-done.2
  28.1 4.6 %shard_map.102 = (bf16[128,1024]{1,0:T(8,128)(2,1)}, bf16[128,1024]{1,0:T(8,128)(2,1)}, bf16[8,128,256]{2,1,0:T(8,128)(2,1)S(1)}) custom-call(s32[1]{0:T(128)} %bitcast.me_ref, bf16[8,128,256]{2,1,0:T(8,128)(2,1)S(1)} %all_to_all.10.kv_ref, bf16[128,1024]{1,0:T(8,128)(2,1)S(1)} %copy-done, bf16[128,1024]{1,0:T(8,128)(2,1)S(1)} %copy-done.1, ...), custom_call_target="tpu_custom_call" | custom-call | flops 1610612736 | bytes 3145728 | tf_op jit(solution)/shard_map/pallas_call | solution.py:97
  32.8 19.7 %all_to_all.11 = bf16[8,128,256]{2,1,0:T(8,128)(2,1)S(1)} all-to-all(bf16[8,128,256]{2,1,0:T(8,128)(2,1)S(1)} %get-tuple-element.9), channel_id=1, replica_groups={{5,6,7,0,1,2,3,4},{13,14,15,8,9,10,11,12},{21,22,23,16,17,18,19,20},{29..., dimensions={0} | all-to-all | bytes 1048576 | tf_op jit(solution)/shard_map/all_to_all | solution.py:132
  52.5 0.3 fusion.1
  52.8 1.9 %collective-permute-start.1 = (bf16[128,256]{1,0:T(8,128)(2,1)S(1)}, bf16[128,256]{1,0:T(8,128)(2,1)S(1)}, u32[]{:S(2)}, u32[]{:S(2)}) collective-permute-start(bf16[128,256]{1,0:T(8,128)(2,1)S(1)} %get-tuple-element.10), channel_id=1, source_target_pairs={{8,0},{9,1},{10,2},{11,3},{12,4},{13,5},{14,6},{15,7},{16,8},{17,9... | collective-permute-start | bytes 196616 | tf_op jit(solution)/shard_map/ppermute | solution.py:147
  54.7 7.0 %collective-permute-done.1 = bf16[128,256]{1,0:T(8,128)(2,1)S(1)} collective-permute-done((bf16[128,256]{1,0:T(8,128)(2,1)S(1)}, bf16[128,256]{1,0:T(8,128)(2,1)S(1)}, u32[]{:S(2)}, u32[]{:S(2)}) %collective-permute-start.1) | collective-permute-done | bytes 65568 | tf_op jit(solution)/shard_map/ppermute | solution.py:147
  61.7 0.6 %fusion.2 = (bf16[128,128]{1,0:T(8,128)(2,1)}, bf16[128,128]{1,0:T(8,128)(2,1)}) fusion(bf16[128,256]{1,0:T(8,128)(2,1)S(1)} %add_convert_fusion), kind=kLoop, calls=%fused_computation.10 | loop fusion | bytes 131072 | tf_op jit(solution)/shard_map/slice | solution.py:150
  (3 shorter events, 0.0 us)
Async XLA Ops:
  0.6 0.8 %copy-start.3 = (bf16[128,128]{1,0:T(8,128)(2,1)S(1)}, bf16[128,128]{1,0:T(8,128)(2,1)}, u32[]{:S(2)}) copy-start(bf16[128,128]{1,0:T(8,128)(2,1)} %param.9) | copy-start | bytes 98308
  1.4 7.0 %collective-permute-start = (bf16[128,256]{1,0:T(8,128)(2,1)S(1)}, bf16[128,256]{1,0:T(8,128)(2,1)S(1)}, u32[]{:S(2)}, u32[]{:S(2)}) collective-permute-start(bf16[128,256]{1,0:T(8,128)(2,1)S(1)} %constant_dynamic-update-slice_fusion), channel_id=1, source_target_pairs={{0,8},{1,9},{2,10},{3,11},{4,12},{5,13},{6,14},{7,15},{8,16},{9,17... | collective-permute-start | bytes 196616 | tf_op jit(solution)/shard_map/ppermute | solution.py:138
  7.1 0.7 %copy-start.4 = (s32[8]{0:T(128)S(1)}, s32[8]{0:T(128)}, u32[]{:S(2)}) copy-start(s32[8]{0:T(128)} %constant.20.clone) | copy-start | bytes 100
  8.6 19.6 %copy-start = (bf16[128,1024]{1,0:T(8,128)(2,1)S(1)}, bf16[128,1024]{1,0:T(8,128)(2,1)}, u32[]{:S(2)}) copy-start(bf16[128,1024]{1,0:T(8,128)(2,1)} %q_ref.1) | copy-start | bytes 786436
  8.6 19.6 %copy-start.1 = (bf16[128,1024]{1,0:T(8,128)(2,1)S(1)}, bf16[128,1024]{1,0:T(8,128)(2,1)}, u32[]{:S(2)}) copy-start(bf16[128,1024]{1,0:T(8,128)(2,1)} %g_ref.1) | copy-start | bytes 786436
  8.6 19.5 %copy-start.2 = (s32[65536]{0:T(1024)S(1)}, s32[65536]{0:T(1024)}, u32[]{:S(2)}) copy-start(s32[65536]{0:T(1024)} %param.11) | copy-start | bytes 786436
  52.8 8.9 %collective-permute-start.1 = (bf16[128,256]{1,0:T(8,128)(2,1)S(1)}, bf16[128,256]{1,0:T(8,128)(2,1)S(1)}, u32[]{:S(2)}, u32[]{:S(2)}) collective-permute-start(bf16[128,256]{1,0:T(8,128)(2,1)S(1)} %get-tuple-element.10), channel_id=1, source_target_pairs={{8,0},{9,1},{10,2},{11,3},{12,4},{13,5},{14,6},{15,7},{16,8},{17,9... | collective-permute-start | bytes 196616 | tf_op jit(solution)/shard_map/ppermute | solution.py:147

commit v3 on v2

v3 whole, which is shorter than its diff:
```python
import math

import jax
import jax.numpy as jnp
from jax import lax
from jax.experimental import pallas as pl
from jax.experimental.pallas import tpu as pltpu
from jax.sharding import PartitionSpec as P

REACH = 8
HEADS = 8
MASKED = -1e30
FIRST = 5
ORDER = tuple((FIRST + k) % REACH for k in range(REACH))
AXES = ("outer", "inner")
MIB = 1024 * 1024
VMEM = pl.BlockSpec(memory_space=pltpu.VMEM)
HBM = pl.BlockSpec(memory_space=pltpu.HBM)


def contract_last(left_op, right_op):
    return lax.dot_general(
        left_op, right_op, (((1,), (1,)), ((), ())), preferred_element_type=jnp.float32
    )


def contract_first(left_op, right_op):
    return lax.dot_general(
        left_op, right_op, (((0,), (0,)), ((), ())), preferred_element_type=jnp.float32
    )


def position():
    me = lax.axis_index("outer") * lax.axis_size("inner") + lax.axis_index("inner")
    return me, lax.rem(me, REACH)


def prepare_kernel(
    k_ref, v_ref, q_ref, g_ref, doc_ref, pack_ref, bias_ref, queries_ref, grads_ref, docs_ref, sems
):
    tokens, width = k_ref.shape
    me, mine = position()
    row = me - mine
    first = pl.multiple_of(jnp.maximum(row - REACH, 0), REACH)
    copies = [
        pltpu.make_async_copy(doc_ref.at[pl.ds(first, 2 * REACH), :], docs_ref, sems.at[0]),
        pltpu.make_async_copy(k_ref, pack_ref.at[:, :width], sems.at[1]),
        pltpu.make_async_copy(v_ref, pack_ref.at[:, width:], sems.at[2]),
        pltpu.make_async_copy(q_ref, queries_ref, sems.at[3]),
        pltpu.make_async_copy(g_ref, grads_ref, sems.at[4]),
    ]
    for copy in copies:
        copy.start()
    lane = lax.broadcasted_iota(jnp.int32, (tokens, tokens), 1)
    line = lax.broadcasted_iota(jnp.int32, (tokens, tokens), 0)
    copies[0].wait()
    query_doc = jnp.broadcast_to(docs_ref[pl.ds(me - first, 1), :], (tokens, tokens)).T
    for k, j in enumerate(ORDER):
        block = jnp.where(j <= mine, row + j, row - REACH + j)
        key_doc = docs_ref[pl.ds(jnp.maximum(block, 0) - first, 1), :]
        reach = jnp.where(block < 0, -tokens, jnp.where(j == mine, 0, tokens))
        visible = (key_doc == query_doc) & (lane <= line + reach)
        bias_ref[:, k * tokens : (k + 1) * tokens] = jnp.where(visible, 0.0, MASKED)
    for copy in copies[1:]:
        copy.wait()


def prepare(keys, values, queries, d_out, docs):
    tokens, width = keys.shape
    return pl.pallas_call(
        prepare_kernel,
        out_shape=(
            pltpu.VMEM((tokens, 2 * width), jnp.bfloat16),
            pltpu.VMEM((tokens, REACH * tokens), jnp.float32),
            pltpu.VMEM(queries.shape, jnp.bfloat16),
            pltpu.VMEM(d_out.shape, jnp.bfloat16),
        ),
        in_specs=[HBM] * 5,
        out_specs=(VMEM,) * 4,
        scratch_shapes=[
            pltpu.VMEM((2 * REACH, tokens), jnp.int32),
            pltpu.SemaphoreType.DMA((5,)),
        ],
        compiler_params=pltpu.CompilerParams(vmem_limit_bytes=16 * MIB),
    )(*[pltpu.with_memory_space_constraint(a, pltpu.HBM) for a in (keys, values, queries, d_out, docs)])


def route_kernel(own_ref, behind_ref, out_ref):
    _, mine = position()
    for k, j in enumerate(ORDER):

        @pl.when(j >= mine)
        def _():
            out_ref[k] = own_ref[...]

        @pl.when(j < mine)
        def _():
            out_ref[k] = behind_ref[...]


def route(own, behind):
    return pl.pallas_call(
        route_kernel,
        out_shape=pltpu.VMEM((REACH, *own.shape), own.dtype),
        in_specs=[VMEM, VMEM],
        out_specs=VMEM,
        compiler_params=pltpu.CompilerParams(vmem_limit_bytes=16 * MIB),
    )(own, behind)


def attention_kernel(
    kv_ref, q_ref, g_ref, bias_ref, out_ref, ds_ref, send_ref, w_ref, rows_ref, grads_ref
):
    tokens, width = kv_ref.shape[1], kv_ref.shape[2] // 2
    span = REACH * tokens
    scale = 1.0 / math.sqrt(width)

    keys = kv_ref[:, :, :width].reshape(span, width)
    values = kv_ref[:, :, width:].reshape(span, width)
    values_one = jnp.concatenate([values, jnp.ones_like(values)], axis=1)

    heads = [
        (slice(h * width, (h + 1) * width), slice(h * tokens, (h + 1) * tokens)) for h in range(HEADS)
    ]
    for cols, rows in heads:
        query = q_ref[:, cols]
        rows_ref[rows, :] = query
        scores = contract_last(query, keys) * (scale * math.log2(math.e)) + bias_ref[...]
        top = jnp.max(scores, axis=1, keepdims=True)
        w_ref[rows, :] = jnp.exp2(scores - top).astype(jnp.bfloat16)
    sums_all = jnp.dot(w_ref[...], values_one, preferred_element_type=jnp.float32)
    deltas = []
    for cols, rows in heads:
        inverse = 1.0 / sums_all[rows, width:]
        output = sums_all[rows, :width] * inverse
        out_ref[:, cols] = output.astype(jnp.bfloat16)
        grad = (g_ref[:, cols].astype(jnp.float32) * (inverse * scale)).astype(jnp.bfloat16)
        grads_ref[rows, :] = grad
        deltas.append(jnp.sum(grad.astype(jnp.float32) * output, axis=1, keepdims=True))
    for (cols, rows), delta in zip(heads, deltas):
        slope = contract_last(grads_ref[rows, :], values) - delta
        ds_ref[rows, :] = (w_ref[rows, :].astype(jnp.float32) * slope).astype(jnp.bfloat16)
    dk = contract_first(rows_ref[...], ds_ref[...])
    dv = contract_first(grads_ref[...], w_ref[...])
    for k in range(REACH):
        at = slice(k * tokens, (k + 1) * tokens)
        send_ref[k, :, :width] = dk[:, at].T.astype(jnp.bfloat16)
        send_ref[k, :, width:] = (dv[:, at].T * (1.0 / scale)).astype(jnp.bfloat16)


def attention(window, queries, d_out, bias):
    tokens, wide = queries.shape
    span = window.shape[0] * tokens
    width = window.shape[2] // 2
    return pl.pallas_call(
        attention_kernel,
        out_shape=(
            jax.ShapeDtypeStruct((tokens, wide), jnp.bfloat16),
            pltpu.VMEM((HEADS * tokens, span), jnp.bfloat16),
            jax.ShapeDtypeStruct(window.shape, jnp.bfloat16),
        ),
        in_specs=[VMEM] * 4,
        out_specs=(VMEM,) * 3,
        scratch_shapes=[
            pltpu.VMEM((HEADS * tokens, span), jnp.bfloat16),
            pltpu.VMEM((HEADS * tokens, width), jnp.bfloat16),
            pltpu.VMEM((HEADS * tokens, width), jnp.bfloat16),
        ],
        compiler_params=pltpu.CompilerParams(vmem_limit_bytes=40 * MIB),
        cost_estimate=pl.CostEstimate(
            flops=10 * HEADS * tokens * span * width,
            bytes_accessed=3 * MIB,
            transcendentals=HEADS * tokens * span,
        ),
    )(window, queries, d_out, bias)


def query_kernel(ds_ref, kv_ref, dq_ref):
    tokens, width = kv_ref.shape[1], kv_ref.shape[2] // 2
    keys = kv_ref[:, :, :width].reshape(REACH * tokens, width)
    dq = jnp.dot(ds_ref[...], keys, preferred_element_type=jnp.float32).astype(jnp.bfloat16)
    for h in range(HEADS):
        dq_ref[:, h * width : (h + 1) * width] = dq[h * tokens : (h + 1) * tokens, :]


def query_grad(score_grad, window):
    tokens, width = window.shape[1], window.shape[2] // 2
    return pl.pallas_call(
        query_kernel,
        out_shape=jax.ShapeDtypeStruct((tokens, HEADS * width), jnp.bfloat16),
        in_specs=[VMEM, VMEM],
        out_specs=VMEM,
        compiler_params=pltpu.CompilerParams(vmem_limit_bytes=16 * MIB),
        cost_estimate=pl.CostEstimate(
            flops=2 * HEADS * tokens * REACH * tokens * width, bytes_accessed=3 * MIB, transcendentals=0
        ),
    )(score_grad, window)


def gather_kernel(terms_ref, passed_ref, owned_ref):
    _, mine = position()
    passed = jnp.zeros(passed_ref.shape, jnp.float32)
    owned = jnp.zeros(owned_ref.shape, jnp.float32)
    for k, j in enumerate(ORDER):
        term = terms_ref[k].astype(jnp.float32)
        passed = passed + jnp.where(j < mine, term, 0.0)
        owned = owned + jnp.where(j < mine, 0.0, term)
    passed_ref[...] = passed.astype(jnp.bfloat16)
    owned_ref[...] = owned


def gather(terms):
    return pl.pallas_call(
        gather_kernel,
        out_shape=(pltpu.VMEM(terms.shape[1:], jnp.bfloat16), pltpu.VMEM(terms.shape[1:], jnp.float32)),
        in_specs=[VMEM],
        out_specs=(VMEM, VMEM),
        compiler_params=pltpu.CompilerParams(vmem_limit_bytes=16 * MIB),
    )(terms)


def body(queries, keys, values, d_out, doc_ids):
    n_inner = lax.axis_size("inner")
    total = lax.axis_size("outer") * n_inner
    tokens, width = keys.shape
    lines = [[start + j for j in ORDER] for start in range(0, n_inner, REACH)]

    def exchange(parts):
        return lax.all_to_all(parts, "inner", 0, 0, axis_index_groups=lines)

    packed, bias, queries, d_out = prepare(keys, values, queries, d_out, doc_ids.reshape(-1, tokens))
    behind = lax.ppermute(packed, AXES, [(i, i + REACH) for i in range(total - REACH)])
    window = exchange(route(packed, behind))
    attended, score_grad, parts = attention(window, queries, d_out, bias)
    passed, owned = gather(exchange(parts))
    passed = lax.ppermute(passed, AXES, [(i, i - REACH) for i in range(REACH, total)])
    grad_queries = query_grad(score_grad, window)
    owned = (owned + passed.astype(jnp.float32)).astype(jnp.bfloat16)
    return (attended, grad_queries, owned[:, :width], owned[:, width:])


def solution(mesh):
    split = P(("outer", "inner"), None)
    return jax.shard_map(
        body,
        mesh=mesh,
        in_specs=(split, split, split, split, P()),
        out_specs=(split, split, split, split),
        check_vma=False,
    )
```

time: 62.6 us -> 61.7 us (0.986)
  Pallas kernels: 4.64 us -> 6.42 us
  local copies, waits for them, and re-layouts: 2.09 us -> 0.63 us
  waiting for transfers between devices: 7.61 us -> 6.87 us
    pallas_call x0 -> x4, Pallas kernels: none -> 2.82 us  [the longest x1 1.41 us: query_grad(): pl.pallas_call(query_kernel, out_shape=jax.ShapeDtypeStruct((tokens, HEAD...]
    unnamed x11 -> x0, local copies, waits for them, and re-layouts: 1.44 us -> none
    pallas_call x1, Pallas kernels: 4.64 us -> 3.6 us  [attention(): pl.pallas_call(attention_kernel, out_shape=(jax.ShapeDtypeStruct((tokens,...]
    ppermute x2, waiting for transfers between devices: 7.61 us -> 6.87 us  [the longest x1 5.56 us: body(): lax.ppermute(passed, AXES, [(i, i - REACH) for i in range(REACH, total)])]
  transfers between devices with their start and end apart: 2 -> 2, of which waited for: 2 -> 2; matrix products, arithmetic and copies ran while one was open for 0% -> 0% of each run, Pallas kernels for 0% -> 2%
where the time goes in v3:
time: 61.7 us; the launch traced here: 61.4 us
  blocking collectives  39.2 us (64%)
  starting transfers between devices  7.61 us (12%)
  waiting for transfers between devices  6.87 us (11%)
  Pallas kernels  6.42 us (10%)
  between operations  0.68 us (1%)
  local copies, waits for them, and re-layouts  0.63 us (1%)
    all_to_all x2, blocking collectives, exchange(): return lax.all_to_all(parts, 'inner', 0, 0, axis_index_groups=lines)  39.2 us
    ppermute x1, starting transfers between devices, body(): lax.ppermute(packed, AXES, [(i, i + REACH) for i in range(total - REACH)])  5.69 us
    ppermute x1, waiting for transfers between devices, body(): lax.ppermute(passed, AXES, [(i, i - REACH) for i in range(REACH, total)])  5.56 us
    pallas_call x1, Pallas kernels, attention(): pl.pallas_call(attention_kernel, out_shape=(jax.ShapeDtypeStruct((tokens,...  3.6 us
    ppermute x1, starting transfers between devices, body(): lax.ppermute(passed, AXES, [(i, i - REACH) for i in range(REACH, total)])  1.92 us
    pallas_call x1, Pallas kernels, query_grad(): pl.pallas_call(query_kernel, out_shape=jax.ShapeDtypeStruct((tokens, HEAD...  1.41 us
    ppermute x1, waiting for transfers between devices, body(): lax.ppermute(packed, AXES, [(i, i + REACH) for i in range(total - REACH)])  1.31 us
  transfers between devices with their start and end apart: 2, of which 2 were waited for; matrix products, arithmetic and copies ran while one was open for 0% of the time, Pallas kernels for 2%

profile of v3, /device:TPU:215, one launch (start us, length us, event | category | flops | bytes accessed | tf_op | source)
XLA Modules:
  0.0 61.4 jit_solution(10967916566758877863)
XLA Ops:
  0.6 1.1 %shard_map.84 = (bf16[128,256]{1,0:T(8,128)(2,1)S(1)}, f32[128,1024]{1,0:T(8,128)S(1)}, bf16[128,1024]{1,0:T(8,128)(2,1)S(1)}, bf16[128,1024]{1,0:T(8,128)(2,1)S(1)}) custom-call(bf16[128,128]{1,0:T(8,128)(2,1)} %k_ref.1, bf16[128,128]{1,0:T(8,128)(2,1)} %v_ref.1, bf16[128,1024]{1,0:T(8,128)(2,1)} %q_ref.1, bf16[128,1024]{1,0:T(8,128)(2,1)} %g_ref.1, ...), custom_call_target="tpu_custom_call" | custom-call | tf_op jit(solution)/shard_map/pallas_call | solution.py:70
  1.8 5.7 %collective-permute-start = (bf16[128,256]{1,0:T(8,128)(2,1)S(1)}, bf16[128,256]{1,0:T(8,128)(2,1)S(1)}, u32[]{:S(2)}, u32[]{:S(2)}) collective-permute-start(bf16[128,256]{1,0:T(8,128)(2,1)S(1)} %get-tuple-element.13.own_ref), channel_id=1, source_target_pairs={{0,8},{1,9},{2,10},{3,11},{4,12},{5,13},{6,14},{7,15},{8,16},{9,17... | collective-permute-start | bytes 196616 | tf_op jit(solution)/shard_map/ppermute | solution.py:232
  7.5 1.3 %collective-permute-done.behind_ref = bf16[128,256]{1,0:T(8,128)(2,1)S(1)} collective-permute-done((bf16[128,256]{1,0:T(8,128)(2,1)S(1)}, bf16[128,256]{1,0:T(8,128)(2,1)S(1)}, u32[]{:S(2)}, u32[]{:S(2)}) %collective-permute-start) | collective-permute-done | bytes 65568 | tf_op jit(solution)/shard_map/ppermute | solution.py:232
  8.8 0.1 shard_map.85
  8.9 19.4 %all_to_all.10.kv_ref = bf16[8,128,256]{2,1,0:T(8,128)(2,1)S(1)} all-to-all(bf16[8,128,256]{2,1,0:T(8,128)(2,1)S(1)} %shard_map.85), channel_id=1, replica_groups={{5,6,7,0,1,2,3,4},{13,14,15,8,9,10,11,12},{21,22,23,16,17,18,19,20},{29..., dimensions={0} | all-to-all | bytes 1048576 | tf_op jit(solution)/shard_map/all_to_all | solution.py:229
  28.3 3.6 %shard_map.86 = (bf16[128,1024]{1,0:T(8,128)(2,1)}, bf16[1024,1024]{1,0:T(8,128)(2,1)S(1)}, bf16[8,128,256]{2,1,0:T(8,128)(2,1)S(1)}) custom-call(bf16[8,128,256]{2,1,0:T(8,128)(2,1)S(1)} %all_to_all.10.kv_ref, bf16[128,1024]{1,0:T(8,128)(2,1)S(1)} %get-tuple-element.14.q_ref, bf16[128,1024]{1,0:T(8,128)(2,1)S(1)} %get-tuple-element.15.g_ref, ...), custom_call_target="tpu_custom_call" | custom-call | flops 1342177280 | bytes 3145728 | tf_op jit(solution)/shard_map/pallas_call | solution.py:155
  31.9 19.8 %all_to_all.11.terms_ref = bf16[8,128,256]{2,1,0:T(8,128)(2,1)S(1)} all-to-all(bf16[8,128,256]{2,1,0:T(8,128)(2,1)S(1)} %get-tuple-element.19), channel_id=1, replica_groups={{5,6,7,0,1,2,3,4},{13,14,15,8,9,10,11,12},{21,22,23,16,17,18,19,20},{29..., dimensions={0} | all-to-all | bytes 1048576 | tf_op jit(solution)/shard_map/all_to_all | solution.py:229
  51.6 0.2 shard_map.88
  51.8 1.9 %collective-permute-start.1 = (bf16[128,256]{1,0:T(8,128)(2,1)S(1)}, bf16[128,256]{1,0:T(8,128)(2,1)S(1)}, u32[]{:S(2)}, u32[]{:S(2)}) collective-permute-start(bf16[128,256]{1,0:T(8,128)(2,1)S(1)} %get-tuple-element.21), channel_id=1, source_target_pairs={{8,0},{9,1},{10,2},{11,3},{12,4},{13,5},{14,6},{15,7},{16,8},{17,9... | collective-permute-start | bytes 196616 | tf_op jit(solution)/shard_map/ppermute | solution.py:236
  53.8 1.4 %shard_map.87 = bf16[128,1024]{1,0:T(8,128)(2,1)} custom-call(bf16[1024,1024]{1,0:T(8,128)(2,1)S(1)} %get-tuple-element.18.ds_ref, bf16[8,128,256]{2,1,0:T(8,128)(2,1)S(1)} %all_to_all.10.kv_ref), custom_call_target="tpu_custom_call" | custom-call | flops 268435456 | bytes 3145728 | tf_op jit(solution)/shard_map/pallas_call | solution.py:188
  55.2 5.6 %collective-permute-done.1 = bf16[128,256]{1,0:T(8,128)(2,1)S(1)} collective-permute-done((bf16[128,256]{1,0:T(8,128)(2,1)S(1)}, bf16[128,256]{1,0:T(8,128)(2,1)S(1)}, u32[]{:S(2)}, u32[]{:S(2)}) %collective-permute-start.1) | collective-permute-done | bytes 65568 | tf_op jit(solution)/shard_map/ppermute | solution.py:236
  60.7 0.6 %fusion = (bf16[128,128]{1,0:T(8,128)(2,1)}, bf16[128,128]{1,0:T(8,128)(2,1)}) fusion(bf16[128,256]{1,0:T(8,128)(2,1)S(1)} %add_convert_fusion), kind=kLoop, calls=%fused_computation.1 | loop fusion | bytes 131072 | tf_op jit(solution)/shard_map/slice | solution.py:239
  (1 shorter events, 0.0 us)
Async XLA Ops:
  1.8 7.0 %collective-permute-start = (bf16[128,256]{1,0:T(8,128)(2,1)S(1)}, bf16[128,256]{1,0:T(8,128)(2,1)S(1)}, u32[]{:S(2)}, u32[]{:S(2)}) collective-permute-start(bf16[128,256]{1,0:T(8,128)(2,1)S(1)} %get-tuple-element.13.own_ref), channel_id=1, source_target_pairs={{0,8},{1,9},{2,10},{3,11},{4,12},{5,13},{6,14},{7,15},{8,16},{9,17... | collective-permute-start | bytes 196616 | tf_op jit(solution)/shard_map/ppermute | solution.py:232
  51.8 8.9 %collective-permute-start.1 = (bf16[128,256]{1,0:T(8,128)(2,1)S(1)}, bf16[128,256]{1,0:T(8,128)(2,1)S(1)}, u32[]{:S(2)}, u32[]{:S(2)}) collective-permute-start(bf16[128,256]{1,0:T(8,128)(2,1)S(1)} %get-tuple-element.21), channel_id=1, source_target_pairs={{8,0},{9,1},{10,2},{11,3},{12,4},{13,5},{14,6},{15,7},{16,8},{17,9... | collective-permute-start | bytes 196616 | tf_op jit(solution)/shard_map/ppermute | solution.py:236

commit v4 on v3

--- a/solution.py
+++ b/solution.py
@@ -35,19 +35,43 @@
     return me, lax.rem(me, REACH)
 
 
-def prepare_kernel(
-    k_ref, v_ref, q_ref, g_ref, doc_ref, pack_ref, bias_ref, queries_ref, grads_ref, docs_ref, sems
-):
-    tokens, width = k_ref.shape
+def on_first_core():
+    return lax.rem(lax.axis_index("outer"), 2) == 0
+
+
+def pack_kernel(k_ref, v_ref, pack_ref, sems):
+    width = k_ref.shape[1]
+    copies = [
+        pltpu.make_async_copy(k_ref, pack_ref.at[:, :width], sems.at[0]),
+        pltpu.make_async_copy(v_ref, pack_ref.at[:, width:], sems.at[1]),
+    ]
+    for copy in copies:
+        copy.start()
+    for copy in copies:
+        copy.wait()
+
+
+def pack(keys, values):
+    tokens, width = keys.shape
+    return pl.pallas_call(
+        pack_kernel,
+        out_shape=pltpu.VMEM((tokens, 2 * width), jnp.bfloat16),
+        in_specs=[HBM] * 2,
+        out_specs=VMEM,
+        scratch_shapes=[pltpu.SemaphoreType.DMA((2,))],
+        compiler_params=pltpu.CompilerParams(vmem_limit_bytes=16 * MIB),
+    )(*[pltpu.with_memory_space_constraint(a, pltpu.HBM) for a in (keys, values)])
+
+
+def stage(q_ref, g_ref, doc_ref, bias_ref, queries_ref, grads_ref, turned_ref, docs_ref, sems):
+    tokens = bias_ref.shape[0]
     me, mine = position()
     row = me - mine
     first = pl.multiple_of(jnp.maximum(row - REACH, 0), REACH)
     copies = [
         pltpu.make_async_copy(doc_ref.at[pl.ds(first, 2 * REACH), :], docs_ref, sems.at[0]),
-        pltpu.make_async_copy(k_ref, pack_ref.at[:, :width], sems.at[1]),
-        pltpu.make_async_copy(v_ref, pack_ref.at[:, width:], sems.at[2]),
-        pltpu.make_async_copy(q_ref, queries_ref, sems.at[3]),
-        pltpu.make_async_copy(g_ref, grads_ref, sems.at[4]),
+        pltpu.make_async_copy(q_ref, queries_ref, sems.at[1]),
+        pltpu.make_async_copy(g_ref, grads_ref, sems.at[2]),
     ]
     for copy in copies:
         copy.start()
@@ -63,29 +87,38 @@
         bias_ref[:, k * tokens : (k + 1) * tokens] = jnp.where(visible, 0.0, MASKED)
     for copy in copies[1:]:
         copy.wait()
-
-
-def prepare(keys, values, queries, d_out, docs):
-    tokens, width = keys.shape
+    width = turned_ref.shape[0]
+    for h in range(HEADS):
+        turned_ref[:, h * tokens : (h + 1) * tokens] = queries_ref[:, h * width : (h + 1) * width].T
+
+
+def prepare_kernel(*refs):
+    @pl.when(jnp.logical_not(on_first_core()))
+    def _():
+        stage(*refs)
+
+
+def prepare(queries, d_out, docs):
+    tokens = queries.shape[0]
     return pl.pallas_call(
         prepare_kernel,
         out_shape=(
-            pltpu.VMEM((tokens, 2 * width), jnp.bfloat16),
             pltpu.VMEM((tokens, REACH * tokens), jnp.float32),
             pltpu.VMEM(queries.shape, jnp.bfloat16),
             pltpu.VMEM(d_out.shape, jnp.bfloat16),
-        ),
-        in_specs=[HBM] * 5,
+            pltpu.VMEM((queries.shape[1] // HEADS, HEADS * tokens), jnp.bfloat16),
+        ),
+        in_specs=[HBM] * 3,
         out_specs=(VMEM,) * 4,
         scratch_shapes=[
             pltpu.VMEM((2 * REACH, tokens), jnp.int32),
-            pltpu.SemaphoreType.DMA((5,)),
+            pltpu.SemaphoreType.DMA((3,)),
         ],
         compiler_params=pltpu.CompilerParams(vmem_limit_bytes=16 * MIB),
-    )(*[pltpu.with_memory_space_constraint(a, pltpu.HBM) for a in (keys, values, queries, d_out, docs)])
-
-
-def route_kernel(own_ref, behind_ref, out_ref):
+    )(*[pltpu.with_memory_space_constraint(a, pltpu.HBM) for a in (queries, d_out, docs)])
+
+
+def route_kernel(own_ref, behind_ref, q_ref, g_ref, doc_ref, b_in, q_in, g_in, t_in, out_ref, *refs):
     _, mine = position()
     for k, j in enumerate(ORDER):
 
@@ -97,19 +130,32 @@
         def _():
             out_ref[k] = behind_ref[...]
 
-
-def route(own, behind):
+    @pl.when(on_first_core())
+    def _():
+        stage(q_ref, g_ref, doc_ref, *refs)
+
+
+def route(own, behind, queries, d_out, docs, staged):
+    tokens = own.shape[0]
     return pl.pallas_call(
         route_kernel,
-        out_shape=pltpu.VMEM((REACH, *own.shape), own.dtype),
-        in_specs=[VMEM, VMEM],
-        out_specs=VMEM,
-        compiler_params=pltpu.CompilerParams(vmem_limit_bytes=16 * MIB),
-    )(own, behind)
+        out_shape=(
+            pltpu.VMEM((REACH, *own.shape), own.dtype),
+            *[pltpu.VMEM(a.shape, a.dtype) for a in staged],
+        ),
+        in_specs=[VMEM] * 2 + [HBM] * 3 + [VMEM] * 4,
+        out_specs=(VMEM,) * 5,
+        input_output_aliases={5: 1, 6: 2, 7: 3, 8: 4},
+        scratch_shapes=[
+            pltpu.VMEM((2 * REACH, tokens), jnp.int32),
+            pltpu.SemaphoreType.DMA((3,)),
+        ],
+        compiler_params=pltpu.CompilerParams(vmem_limit_bytes=16 * MIB),
+    )(own, behind, *[pltpu.with_memory_space_constraint(a, pltpu.HBM) for a in (queries, d_out, docs)], *staged)
 
 
 def attention_kernel(
-    kv_ref, q_ref, g_ref, bias_ref, out_ref, ds_ref, send_ref, w_ref, rows_ref, grads_ref
+    kv_ref, q_ref, g_ref, bias_ref, turned_ref, out_ref, ds_ref, send_ref, w_ref, grads_ref
 ):
     tokens, width = kv_ref.shape[1], kv_ref.shape[2] // 2
     span = REACH * tokens
@@ -124,7 +170,6 @@
     ]
     for cols, rows in heads:
         query = q_ref[:, cols]
-        rows_ref[rows, :] = query
         scores = contract_last(query, keys) * (scale * math.log2(math.e)) + bias_ref[...]
         top = jnp.max(scores, axis=1, keepdims=True)
         w_ref[rows, :] = jnp.exp2(scores - top).astype(jnp.bfloat16)
@@ -140,7 +185,7 @@
     for (cols, rows), delta in zip(heads, deltas):
         slope = contract_last(grads_ref[rows, :], values) - delta
         ds_ref[rows, :] = (w_ref[rows, :].astype(jnp.float32) * slope).astype(jnp.bfloat16)
-    dk = contract_first(rows_ref[...], ds_ref[...])
+    dk = jnp.dot(turned_ref[...], ds_ref[...], preferred_element_type=jnp.float32)
     dv = contract_first(grads_ref[...], w_ref[...])
     for k in range(REACH):
         at = slice(k * tokens, (k + 1) * tokens)
@@ -148,7 +193,7 @@
         send_ref[k, :, width:] = (dv[:, at].T * (1.0 / scale)).astype(jnp.bfloat16)
 
 
-def attention(window, queries, d_out, bias):
+def attention(window, queries, d_out, bias, turned):
     tokens, wide = queries.shape
     span = window.shape[0] * tokens
     width = window.shape[2] // 2
@@ -159,11 +204,10 @@
             pltpu.VMEM((HEADS * tokens, span), jnp.bfloat16),
             jax.ShapeDtypeStruct(window.shape, jnp.bfloat16),
         ),
-        in_specs=[VMEM] * 4,
+        in_specs=[VMEM] * 5,
         out_specs=(VMEM,) * 3,
         scratch_shapes=[
             pltpu.VMEM((HEADS * tokens, span), jnp.bfloat16),
-            pltpu.VMEM((HEADS * tokens, width), jnp.bfloat16),
             pltpu.VMEM((HEADS * tokens, width), jnp.bfloat16),
         ],
         compiler_params=pltpu.CompilerParams(vmem_limit_bytes=40 * MIB),
@@ -172,7 +216,7 @@
             bytes_accessed=3 * MIB,
             transcendentals=HEADS * tokens * span,
         ),
-    )(window, queries, d_out, bias)
+    )(window, queries, d_out, bias, turned)
 
 
 def query_kernel(ds_ref, kv_ref, dq_ref):
@@ -188,7 +232,7 @@
     return pl.pallas_call(
         query_kernel,
         out_shape=jax.ShapeDtypeStruct((tokens, HEADS * width), jnp.bfloat16),
-        in_specs=[VMEM, VMEM],
+        in_specs=[VMEM] * 2,
         out_specs=VMEM,
         compiler_params=pltpu.CompilerParams(vmem_limit_bytes=16 * MIB),
         cost_estimate=pl.CostEstimate(
@@ -228,10 +272,14 @@
     def exchange(parts):
         return lax.all_to_all(parts, "inner", 0, 0, axis_index_groups=lines)
 
-    packed, bias, queries, d_out = prepare(keys, values, queries, d_out, doc_ids.reshape(-1, tokens))
+    packed = pack(keys, values)
     behind = lax.ppermute(packed, AXES, [(i, i + REACH) for i in range(total - REACH)])
-    window = exchange(route(packed, behind))
-    attended, score_grad, parts = attention(window, queries, d_out, bias)
+    docs = doc_ids.reshape(-1, tokens)
+    staged = prepare(queries, d_out, docs)
+    behind, *staged = lax.optimization_barrier((behind, *staged))
+    outgoing, bias, rows, grads, turned = route(packed, behind, queries, d_out, docs, staged)
+    window = exchange(outgoing)
+    attended, score_grad, parts = attention(window, rows, grads, bias, turned)
     passed, owned = gather(exchange(parts))
     passed = lax.ppermute(passed, AXES, [(i, i - REACH) for i in range(REACH, total)])
     grad_queries = query_grad(score_grad, window)

time: 61.7 us -> 58.5 us (0.948)
  the two profiles are of different devices: /device:TPU:215 before, /device:TPU:238 now
where the time goes in v4:
time: 58.5 us; the launch traced here: 58.2 us
  blocking collectives  38.2 us (65%)
  waiting for transfers between devices  7.63 us (13%)
  Pallas kernels  7.23 us (12%)
  starting transfers between devices  3.84 us (7%)
  between operations  0.69 us (1%)
  local copies, waits for them, and re-layouts  0.63 us (1%)
    all_to_all x2, blocking collectives, exchange(): return lax.all_to_all(parts, 'inner', 0, 0, axis_index_groups=lines)  38.2 us
    ppermute x1, waiting for transfers between devices, body(): lax.ppermute(packed, AXES, [(i, i + REACH) for i in range(total - REACH)])  4.18 us
    pallas_call x1, Pallas kernels, attention(): pl.pallas_call(attention_kernel, out_shape=(jax.ShapeDtypeStruct((tokens,...  3.52 us
    ppermute x1, waiting for transfers between devices, body(): lax.ppermute(passed, AXES, [(i, i - REACH) for i in range(REACH, total)])  3.45 us
    ppermute x1, starting transfers between devices, body(): lax.ppermute(packed, AXES, [(i, i + REACH) for i in range(total - REACH)])  1.92 us
    ppermute x1, starting transfers between devices, body(): lax.ppermute(passed, AXES, [(i, i - REACH) for i in range(REACH, total)])  1.92 us
    pallas_call x1, Pallas kernels, query_grad(): pl.pallas_call(query_kernel, out_shape=jax.ShapeDtypeStruct((tokens, HEAD...  1.41 us
    pallas_call x1, Pallas kernels, route(): pl.pallas_call(route_kernel, out_shape=(pltpu.VMEM((REACH, *own.shape), o...  1.26 us
  transfers between devices with their start and end apart: 2, of which 2 were waited for; matrix products, arithmetic and copies ran while one was open for 0% of the time, Pallas kernels for 3%

profile of v4, /device:TPU:238, one launch (start us, length us, event | category | flops | bytes accessed | tf_op | source)
XLA Modules:
  0.0 58.2 jit_solution(14954571420957803014)
XLA Ops:
  0.6 0.8 %shard_map.84.own_ref = bf16[128,256]{1,0:T(8,128)(2,1)S(1)} custom-call(bf16[128,128]{1,0:T(8,128)(2,1)} %k_ref.1, bf16[128,128]{1,0:T(8,128)(2,1)} %v_ref.1), custom_call_target="tpu_custom_call" | custom-call | tf_op jit(solution)/shard_map/pallas_call | solution.py:56
  1.4 1.9 %collective-permute-start = (bf16[128,256]{1,0:T(8,128)(2,1)S(1)}, bf16[128,256]{1,0:T(8,128)(2,1)S(1)}, u32[]{:S(2)}, u32[]{:S(2)}) collective-permute-start(bf16[128,256]{1,0:T(8,128)(2,1)S(1)} %shard_map.84.own_ref), channel_id=1, source_target_pairs={{0,8},{1,9},{2,10},{3,11},{4,12},{5,13},{6,14},{7,15},{8,16},{9,17... | collective-permute-start | bytes 196616 | tf_op jit(solution)/shard_map/ppermute | solution.py:276
  3.4 4.2 %collective-permute-done.behind_ref = bf16[128,256]{1,0:T(8,128)(2,1)S(1)} collective-permute-done((bf16[128,256]{1,0:T(8,128)(2,1)S(1)}, bf16[128,256]{1,0:T(8,128)(2,1)S(1)}, u32[]{:S(2)}, u32[]{:S(2)}) %collective-permute-start) | collective-permute-done | bytes 65568 | tf_op jit(solution)/shard_map/ppermute | solution.py:276
  7.6 1.3 %shard_map.86 = (bf16[8,128,256]{2,1,0:T(8,128)(2,1)S(1)}, f32[128,1024]{1,0:T(8,128)S(1)}, bf16[128,1024]{1,0:T(8,128)(2,1)S(1)}, bf16[128,1024]{1,0:T(8,128)(2,1)S(1)}, bf16[128,1024]{1,0:T(8,128)(2,1)S(1)}) custom-call(bf16[128,256]{1,0:T(8,128)(2,1)S(1)} %shard_map.84.own_ref, ...), custom_call_target="tpu_custom_call", output_to_operand_aliasing={{1}: (5, {}), {2}: (6, {}), {3}: (7, {}), {4}: (8, {})} | custom-call | tf_op jit(solution)/shard_map/pallas_call | solution.py:140
  8.9 19.9 %all_to_all.10.kv_ref = bf16[8,128,256]{2,1,0:T(8,128)(2,1)S(1)} all-to-all(bf16[8,128,256]{2,1,0:T(8,128)(2,1)S(1)} %get-tuple-element.32), channel_id=1, replica_groups={{5,6,7,0,1,2,3,4},{13,14,15,8,9,10,11,12},{21,22,23,16,17,18,19,20},{29..., dimensions={0} | all-to-all | bytes 1048576 | tf_op jit(solution)/shard_map/all_to_all | solution.py:273
  28.7 3.5 %shard_map.87 = (bf16[128,1024]{1,0:T(8,128)(2,1)}, bf16[1024,1024]{1,0:T(8,128)(2,1)S(1)}, bf16[8,128,256]{2,1,0:T(8,128)(2,1)S(1)}) custom-call(bf16[8,128,256]{2,1,0:T(8,128)(2,1)S(1)} %all_to_all.10.kv_ref, bf16[128,1024]{1,0:T(8,128)(2,1)S(1)} %get-tuple-element.33.q_ref, bf16[128,1024]{1,0:T(8,128)(2,1)S(1)} %get-tuple-element.34.g_ref, ...), custom_call_target="tpu_custom_call" | custom-call | flops 1342177280 | bytes 3145728 | tf_op jit(solution)/shard_map/pallas_call | solution.py:200
  32.2 18.3 %all_to_all.11.terms_ref = bf16[8,128,256]{2,1,0:T(8,128)(2,1)S(1)} all-to-all(bf16[8,128,256]{2,1,0:T(8,128)(2,1)S(1)} %get-tuple-element.39), channel_id=1, replica_groups={{5,6,7,0,1,2,3,4},{13,14,15,8,9,10,11,12},{21,22,23,16,17,18,19,20},{29..., dimensions={0} | all-to-all | bytes 1048576 | tf_op jit(solution)/shard_map/all_to_all | solution.py:273
  50.6 0.2 shard_map.89
  50.8 1.9 %collective-permute-start.1 = (bf16[128,256]{1,0:T(8,128)(2,1)S(1)}, bf16[128,256]{1,0:T(8,128)(2,1)S(1)}, u32[]{:S(2)}, u32[]{:S(2)}) collective-permute-start(bf16[128,256]{1,0:T(8,128)(2,1)S(1)} %get-tuple-element.41), channel_id=1, source_target_pairs={{8,0},{9,1},{10,2},{11,3},{12,4},{13,5},{14,6},{15,7},{16,8},{17,9... | collective-permute-start | bytes 196616 | tf_op jit(solution)/shard_map/ppermute | solution.py:284
  52.7 1.4 %shard_map.88 = bf16[128,1024]{1,0:T(8,128)(2,1)} custom-call(bf16[1024,1024]{1,0:T(8,128)(2,1)S(1)} %get-tuple-element.38.ds_ref, bf16[8,128,256]{2,1,0:T(8,128)(2,1)S(1)} %all_to_all.10.kv_ref), custom_call_target="tpu_custom_call" | custom-call | flops 268435456 | bytes 3145728 | tf_op jit(solution)/shard_map/pallas_call | solution.py:232
  54.1 3.5 %collective-permute-done.1 = bf16[128,256]{1,0:T(8,128)(2,1)S(1)} collective-permute-done((bf16[128,256]{1,0:T(8,128)(2,1)S(1)}, bf16[128,256]{1,0:T(8,128)(2,1)S(1)}, u32[]{:S(2)}, u32[]{:S(2)}) %collective-permute-start.1) | collective-permute-done | bytes 65568 | tf_op jit(solution)/shard_map/ppermute | solution.py:284
  57.6 0.6 %fusion = (bf16[128,128]{1,0:T(8,128)(2,1)}, bf16[128,128]{1,0:T(8,128)(2,1)}) fusion(bf16[128,256]{1,0:T(8,128)(2,1)S(1)} %add_convert_fusion), kind=kLoop, calls=%fused_computation.1 | loop fusion | bytes 131072 | tf_op jit(solution)/shard_map/slice | solution.py:287
  (2 shorter events, 0.1 us)
Async XLA Ops:
  1.4 6.2 %collective-permute-start = (bf16[128,256]{1,0:T(8,128)(2,1)S(1)}, bf16[128,256]{1,0:T(8,128)(2,1)S(1)}, u32[]{:S(2)}, u32[]{:S(2)}) collective-permute-start(bf16[128,256]{1,0:T(8,128)(2,1)S(1)} %shard_map.84.own_ref), channel_id=1, source_target_pairs={{0,8},{1,9},{2,10},{3,11},{4,12},{5,13},{6,14},{7,15},{8,16},{9,17... | collective-permute-start | bytes 196616 | tf_op jit(solution)/shard_map/ppermute | solution.py:276
  50.8 6.8 %collective-permute-start.1 = (bf16[128,256]{1,0:T(8,128)(2,1)S(1)}, bf16[128,256]{1,0:T(8,128)(2,1)S(1)}, u32[]{:S(2)}, u32[]{:S(2)}) collective-permute-start(bf16[128,256]{1,0:T(8,128)(2,1)S(1)} %get-tuple-element.41), channel_id=1, source_target_pairs={{8,0},{9,1},{10,2},{11,3},{12,4},{13,5},{14,6},{15,7},{16,8},{17,9... | collective-permute-start | bytes 196616 | tf_op jit(solution)/shard_map/ppermute | solution.py:284

commit v5 on v4

--- a/solution.py
+++ b/solution.py
@@ -155,7 +155,7 @@
 
 
 def attention_kernel(
-    kv_ref, q_ref, g_ref, bias_ref, turned_ref, out_ref, ds_ref, send_ref, w_ref, grads_ref
+    kv_ref, q_ref, g_ref, bias_ref, turned_ref, out_ref, ds_ref, send_ref, w_ref, grads_ref, flipped_ref
 ):
     tokens, width = kv_ref.shape[1], kv_ref.shape[2] // 2
     span = REACH * tokens
@@ -181,12 +181,13 @@
         out_ref[:, cols] = output.astype(jnp.bfloat16)
         grad = (g_ref[:, cols].astype(jnp.float32) * (inverse * scale)).astype(jnp.bfloat16)
         grads_ref[rows, :] = grad
+        flipped_ref[:, rows] = grad.T
         deltas.append(jnp.sum(grad.astype(jnp.float32) * output, axis=1, keepdims=True))
     for (cols, rows), delta in zip(heads, deltas):
         slope = contract_last(grads_ref[rows, :], values) - delta
         ds_ref[rows, :] = (w_ref[rows, :].astype(jnp.float32) * slope).astype(jnp.bfloat16)
     dk = jnp.dot(turned_ref[...], ds_ref[...], preferred_element_type=jnp.float32)
-    dv = contract_first(grads_ref[...], w_ref[...])
+    dv = jnp.dot(flipped_ref[...], w_ref[...], preferred_element_type=jnp.float32)
     for k in range(REACH):
         at = slice(k * tokens, (k + 1) * tokens)
         send_ref[k, :, :width] = dk[:, at].T.astype(jnp.bfloat16)
@@ -209,6 +210,7 @@
         scratch_shapes=[
             pltpu.VMEM((HEADS * tokens, span), jnp.bfloat16),
             pltpu.VMEM((HEADS * tokens, width), jnp.bfloat16),
+            pltpu.VMEM((width, HEADS * tokens), jnp.bfloat16),
         ],
         compiler_params=pltpu.CompilerParams(vmem_limit_bytes=40 * MIB),
         cost_estimate=pl.CostEstimate(

time: 58.5 us -> 58.5 us (level)
  no operation moved by 1% of the time
where the time goes in v5:
time: 58.5 us; the launch traced here: 58.2 us
  blocking collectives  38.2 us (65%)
  waiting for transfers between devices  7.63 us (13%)
  Pallas kernels  7.23 us (12%)
  starting transfers between devices  3.84 us (7%)
  between operations  0.69 us (1%)
  local copies, waits for them, and re-layouts  0.63 us (1%)
    all_to_all x2, blocking collectives, exchange(): return lax.all_to_all(parts, 'inner', 0, 0, axis_index_groups=lines)  38.2 us
    ppermute x1, waiting for transfers between devices, body(): lax.ppermute(packed, AXES, [(i, i + REACH) for i in range(total - REACH)])  4.18 us
    pallas_call x1, Pallas kernels, attention(): pl.pallas_call(attention_kernel, out_shape=(jax.ShapeDtypeStruct((tokens,...  3.52 us
    ppermute x1, waiting for transfers between devices, body(): lax.ppermute(passed, AXES, [(i, i - REACH) for i in range(REACH, total)])  3.46 us
    ppermute x1, starting transfers between devices, body(): lax.ppermute(packed, AXES, [(i, i + REACH) for i in range(total - REACH)])  1.92 us
    ppermute x1, starting transfers between devices, body(): lax.ppermute(passed, AXES, [(i, i - REACH) for i in range(REACH, total)])  1.92 us
    pallas_call x1, Pallas kernels, query_grad(): pl.pallas_call(query_kernel, out_shape=jax.ShapeDtypeStruct((tokens, HEAD...  1.41 us
    pallas_call x1, Pallas kernels, route(): pl.pallas_call(route_kernel, out_shape=(pltpu.VMEM((REACH, *own.shape), o...  1.26 us
  transfers between devices with their start and end apart: 2, of which 2 were waited for; matrix products, arithmetic and copies ran while one was open for 0% of the time, Pallas kernels for 3%

profile of v5, /device:TPU:238, one launch (start us, length us, event | category | flops | bytes accessed | tf_op | source)
XLA Modules:
  0.0 58.2 jit_solution(5634201332468257923)
XLA Ops:
  0.6 0.8 %shard_map.84.own_ref = bf16[128,256]{1,0:T(8,128)(2,1)S(1)} custom-call(bf16[128,128]{1,0:T(8,128)(2,1)} %k_ref.1, bf16[128,128]{1,0:T(8,128)(2,1)} %v_ref.1), custom_call_target="tpu_custom_call" | custom-call | tf_op jit(solution)/shard_map/pallas_call | solution.py:56
  1.4 1.9 %collective-permute-start = (bf16[128,256]{1,0:T(8,128)(2,1)S(1)}, bf16[128,256]{1,0:T(8,128)(2,1)S(1)}, u32[]{:S(2)}, u32[]{:S(2)}) collective-permute-start(bf16[128,256]{1,0:T(8,128)(2,1)S(1)} %shard_map.84.own_ref), channel_id=1, source_target_pairs={{0,8},{1,9},{2,10},{3,11},{4,12},{5,13},{6,14},{7,15},{8,16},{9,17... | collective-permute-start | bytes 196616 | tf_op jit(solution)/shard_map/ppermute | solution.py:278
  3.4 4.2 %collective-permute-done.behind_ref = bf16[128,256]{1,0:T(8,128)(2,1)S(1)} collective-permute-done((bf16[128,256]{1,0:T(8,128)(2,1)S(1)}, bf16[128,256]{1,0:T(8,128)(2,1)S(1)}, u32[]{:S(2)}, u32[]{:S(2)}) %collective-permute-start) | collective-permute-done | bytes 65568 | tf_op jit(solution)/shard_map/ppermute | solution.py:278
  7.6 1.3 %shard_map.86 = (bf16[8,128,256]{2,1,0:T(8,128)(2,1)S(1)}, f32[128,1024]{1,0:T(8,128)S(1)}, bf16[128,1024]{1,0:T(8,128)(2,1)S(1)}, bf16[128,1024]{1,0:T(8,128)(2,1)S(1)}, bf16[128,1024]{1,0:T(8,128)(2,1)S(1)}) custom-call(bf16[128,256]{1,0:T(8,128)(2,1)S(1)} %shard_map.84.own_ref, ...), custom_call_target="tpu_custom_call", output_to_operand_aliasing={{1}: (5, {}), {2}: (6, {}), {3}: (7, {}), {4}: (8, {})} | custom-call | tf_op jit(solution)/shard_map/pallas_call | solution.py:140
  8.9 19.9 %all_to_all.10.kv_ref = bf16[8,128,256]{2,1,0:T(8,128)(2,1)S(1)} all-to-all(bf16[8,128,256]{2,1,0:T(8,128)(2,1)S(1)} %get-tuple-element.32), channel_id=1, replica_groups={{5,6,7,0,1,2,3,4},{13,14,15,8,9,10,11,12},{21,22,23,16,17,18,19,20},{29..., dimensions={0} | all-to-all | bytes 1048576 | tf_op jit(solution)/shard_map/all_to_all | solution.py:275
  28.7 3.5 %shard_map.87 = (bf16[128,1024]{1,0:T(8,128)(2,1)}, bf16[1024,1024]{1,0:T(8,128)(2,1)S(1)}, bf16[8,128,256]{2,1,0:T(8,128)(2,1)S(1)}) custom-call(bf16[8,128,256]{2,1,0:T(8,128)(2,1)S(1)} %all_to_all.10.kv_ref, bf16[128,1024]{1,0:T(8,128)(2,1)S(1)} %get-tuple-element.33.q_ref, bf16[128,1024]{1,0:T(8,128)(2,1)S(1)} %get-tuple-element.34.g_ref, ...), custom_call_target="tpu_custom_call" | custom-call | flops 1342177280 | bytes 3145728 | tf_op jit(solution)/shard_map/pallas_call | solution.py:201
  32.2 18.3 %all_to_all.11.terms_ref = bf16[8,128,256]{2,1,0:T(8,128)(2,1)S(1)} all-to-all(bf16[8,128,256]{2,1,0:T(8,128)(2,1)S(1)} %get-tuple-element.39), channel_id=1, replica_groups={{5,6,7,0,1,2,3,4},{13,14,15,8,9,10,11,12},{21,22,23,16,17,18,19,20},{29..., dimensions={0} | all-to-all | bytes 1048576 | tf_op jit(solution)/shard_map/all_to_all | solution.py:275
  50.6 0.2 shard_map.89
  50.8 1.9 %collective-permute-start.1 = (bf16[128,256]{1,0:T(8,128)(2,1)S(1)}, bf16[128,256]{1,0:T(8,128)(2,1)S(1)}, u32[]{:S(2)}, u32[]{:S(2)}) collective-permute-start(bf16[128,256]{1,0:T(8,128)(2,1)S(1)} %get-tuple-element.41), channel_id=1, source_target_pairs={{8,0},{9,1},{10,2},{11,3},{12,4},{13,5},{14,6},{15,7},{16,8},{17,9... | collective-permute-start | bytes 196616 | tf_op jit(solution)/shard_map/ppermute | solution.py:286
  52.7 1.4 %shard_map.88 = bf16[128,1024]{1,0:T(8,128)(2,1)} custom-call(bf16[1024,1024]{1,0:T(8,128)(2,1)S(1)} %get-tuple-element.38.ds_ref, bf16[8,128,256]{2,1,0:T(8,128)(2,1)S(1)} %all_to_all.10.kv_ref), custom_call_target="tpu_custom_call" | custom-call | flops 268435456 | bytes 3145728 | tf_op jit(solution)/shard_map/pallas_call | solution.py:234
  54.1 3.5 %collective-permute-done.1 = bf16[128,256]{1,0:T(8,128)(2,1)S(1)} collective-permute-done((bf16[128,256]{1,0:T(8,128)(2,1)S(1)}, bf16[128,256]{1,0:T(8,128)(2,1)S(1)}, u32[]{:S(2)}, u32[]{:S(2)}) %collective-permute-start.1) | collective-permute-done | bytes 65568 | tf_op jit(solution)/shard_map/ppermute | solution.py:286
  57.6 0.6 %fusion = (bf16[128,128]{1,0:T(8,128)(2,1)}, bf16[128,128]{1,0:T(8,128)(2,1)}) fusion(bf16[128,256]{1,0:T(8,128)(2,1)S(1)} %add_convert_fusion), kind=kLoop, calls=%fused_computation.1 | loop fusion | bytes 131072 | tf_op jit(solution)/shard_map/slice | solution.py:289
  (2 shorter events, 0.1 us)
Async XLA Ops:
  1.4 6.2 %collective-permute-start = (bf16[128,256]{1,0:T(8,128)(2,1)S(1)}, bf16[128,256]{1,0:T(8,128)(2,1)S(1)}, u32[]{:S(2)}, u32[]{:S(2)}) collective-permute-start(bf16[128,256]{1,0:T(8,128)(2,1)S(1)} %shard_map.84.own_ref), channel_id=1, source_target_pairs={{0,8},{1,9},{2,10},{3,11},{4,12},{5,13},{6,14},{7,15},{8,16},{9,17... | collective-permute-start | bytes 196616 | tf_op jit(solution)/shard_map/ppermute | solution.py:278
  50.8 6.8 %collective-permute-start.1 = (bf16[128,256]{1,0:T(8,128)(2,1)S(1)}, bf16[128,256]{1,0:T(8,128)(2,1)S(1)}, u32[]{:S(2)}, u32[]{:S(2)}) collective-permute-start(bf16[128,256]{1,0:T(8,128)(2,1)S(1)} %get-tuple-element.41), channel_id=1, source_target_pairs={{8,0},{9,1},{10,2},{11,3},{12,4},{13,5},{14,6},{15,7},{16,8},{17,9... | collective-permute-start | bytes 196616 | tf_op jit(solution)/shard_map/ppermute | solution.py:286
